TPU v7x, 32 devices: a whole 2x2x4 slice. The times are simulated.
32 devices in a mesh: ax: 8 (over y, x, core), vt: 4 (over z).
Axes of the slice: x: 2, y: 2, z: 4, core: 2. Of those that a mesh axis runs over, the one named last changes fastest.
Arguments:
- fractions: float32 [2, 4, 4096, 128], P(None, 'vt', 'ax'), may hold values from 0 to 0.8
- motion_fields: float32 [4, 4, 4096, 128], P(None, 'vt', 'ax'), may hold values from -4 to 4
- new_home: int32 [4, 4096], P('vt', 'ax'), may hold values from 0 to 16383, as said below
- counts: int32 [4, 4096], P('vt', 'ax'), may hold values from 64 to 128, as said below
- neighbours: int32 [6, 4, 4096], P(None, 'vt', 'ax'), may hold values from -1 to 16383, as said below
- phase_ids: int32 [4, 4096, 128], P('vt', 'ax'), may hold values from 0 to 3
- growth_rates: float32 [4], replicated, may hold values from 0.5 to 5
Outputs:
- fractions_out: float32 [2, 4, 4096, 128], P(None, 'vt', 'ax')
- motion_out: float32 [4, 4, 4096, 128], P(None, 'vt', 'ax')
Inputs may be any that keep to these rules, and one draw needn't show every extreme that they name: new_home is a permutation. A block keeps its slot, or moves to the slot with the same vertical index on the device whose ax index is one higher or one lower; a block that leaves a device is replaced in its slot by a block coming from the device it went to. At most 16 blocks pass from one device to one axial neighbour, and in every draw some pair of axially adjacent devices trades exactly 16 blocks each way. `neighbours`: -1 marks a pipe wall. The block across a face lies on a device whose ax index and whose vt index each differ by at most one from those of the block's own device; the relation is symmetric under opposite faces. A device's slots are numbered layer by layer along the pipe, 64 to a layer. Outside a device's lowest layer of slots at most 16 of its blocks have a block across some face on the device whose ax index is one lower, and outside its highest layer at most 16 have one on the device whose ax index is one higher; in every draw some device reaches 16 in each of these. The live cells of a block are its first counts cells; slot 0 of every device holds a full block.
All inputs are finite; a program needn't handle non-finite values.
Results may differ from a plain program's by a relative error of at most 0.0003.
Values sent between devices are 32-bit elements; how exact they have to be, the bound alone decides.
A program may use at most 128 MiB of HBM per device.

v0:
```python
import jax
import jax.numpy as jnp
from jax import lax
from jax.sharding import PartitionSpec as P

MOVES = 16


axis_stride = (1, 32, 8)
axis_extent = (8, 4, 4)
time_step = 0.25


def shifted(value, axis, steps):
    count = lax.axis_size(axis)
    first, last = (max(0, -steps), min(count, count - steps))
    return lax.ppermute(value, axis, [(source, source + steps) for source in range(first, last)])


def with_halo(x, sides, width):
    for axis, dim in sides:
        count, length = (lax.axis_size(axis), x.shape[dim])
        up = [(i, (i + 1) % count) for i in range(count - 1)]
        down = [(j, i) for i, j in up]
        last = lax.slice_in_dim(x, length - width, length, axis=dim)
        first = lax.slice_in_dim(x, 0, width, axis=dim)
        before = lax.ppermute(last, axis, up)
        after = lax.ppermute(first, axis, down)
        x = jnp.concatenate([before, x, after], axis=dim)
    return x


def face_flux(value, other, speed, other_speed, weight, outward_sign):
    outward = outward_sign * 0.5 * (speed + other_speed)
    return weight * (jnp.maximum(outward, 0.0) * value + jnp.minimum(outward, 0.0) * other)


def needed_members(direction):
    return (0, 1, 2 + direction // 2, 5)


def pack_movers(block_cells, leaving, target_slot):
    slot_count = leaving.shape[0]
    earlier = leaving[None, :] & (target_slot[None, :] < target_slot[:, None])
    placing = jnp.sum(earlier.astype(jnp.int32), axis=1)
    wanted = jnp.arange(MOVES, dtype=jnp.int32)[:, None]
    picked = leaving[None, :] & (placing[None, :] == wanted)
    source = jnp.sum(jnp.where(picked, jnp.arange(slot_count, dtype=jnp.int32)[None, :], 0), axis=1)
    filled = jnp.any(picked, axis=1)
    packed = jnp.take(block_cells, source, axis=1)
    return jnp.where(filled[None, :, None], packed, 0.0)


def across(own, other, direction):
    along = direction // 2
    stride = axis_stride[along]
    extent = axis_extent[along]
    coordinate = jnp.arange(128, dtype=jnp.int32) // stride % extent
    if direction % 2 == 1:
        inside = jnp.roll(own, -stride, axis=-1)
        from_other = jnp.roll(other, (extent - 1) * stride, axis=-1)
        on_edge = coordinate == extent - 1
    else:
        inside = jnp.roll(own, stride, axis=-1)
        from_other = jnp.roll(other, -(extent - 1) * stride, axis=-1)
        on_edge = coordinate == 0
    return jnp.where(on_edge[None, :], from_other, inside)


def pick_blocks(ghost_blocks, source, row_low, axial_low, axial_count, neighbour_at):
    layer_of, axial_of, slot_of, present = neighbour_at
    slot_count = ghost_blocks.shape[2]
    row_count = source.shape[1]
    flattened = source.reshape(source.shape[0], -1, source.shape[-1])
    row_at = layer_of - row_low
    axial_at = axial_of - axial_low
    usable = (
        present & (row_at >= 0) & (row_at < row_count) & (axial_at >= 0) & (axial_at < axial_count)
    )
    window_index = jnp.clip(
        (row_at * axial_count + axial_at) * slot_count + slot_of, 0, flattened.shape[1] - 1
    )
    updated = []
    for direction in range(6):
        picked = window_index[direction]
        taken = jnp.stack(
            [jnp.take(flattened[member], picked, axis=0) for member in needed_members(direction)]
        )
        updated.append(jnp.where(usable[direction][None, :, None], taken, ghost_blocks[direction]))
    return jnp.stack(updated)


def on_device(fractions, motion_fields, new_home, counts, neighbours, phase_ids, growth_rates):
    axial_size = lax.axis_size("ax")
    my_axial = lax.axis_index("ax")
    my_layer = lax.axis_index("vt")
    slot_count = fractions.shape[2]
    all_slots = slot_count * axial_size
    block_cells = jnp.concatenate([fractions[:, 0], motion_fields[:, 0]], axis=0)
    target = new_home[0]
    target_axial = target % all_slots // slot_count
    target_slot = target % slot_count
    going_up = target_axial == my_axial + 1
    going_down = target_axial == my_axial - 1
    from_below = shifted(pack_movers(block_cells, going_up, target_slot), "ax", 1)
    from_above = shifted(pack_movers(block_cells, going_down, target_slot), "ax", -1)
    up_order = jnp.clip(jnp.cumsum(going_up.astype(jnp.int32)) - 1, 0, MOVES - 1)
    down_order = jnp.clip(jnp.cumsum(going_down.astype(jnp.int32)) - 1, 0, MOVES - 1)
    arrived = jnp.where(
        going_up[None, :, None],
        jnp.take(from_above, up_order, axis=1),
        jnp.where(going_down[None, :, None], jnp.take(from_below, down_order, axis=1), block_cells),
    )
    position = jnp.arange(128, dtype=jnp.int32)
    live_cells = (position[None, :] < counts[0][:, None]).astype(jnp.float32)
    liquid = arrived[0]
    hydrate = arrived[1]
    velocity = arrived[2:5]
    quantities = jnp.stack([liquid, hydrate, velocity[0], velocity[1], velocity[2], live_cells])
    block_data = quantities[:, None]
    linked = neighbours[:, 0]
    present = linked >= 0
    clipped = jnp.maximum(linked, 0)
    neighbour_at = (
        clipped // all_slots,
        clipped % all_slots // slot_count,
        clipped % slot_count,
        present,
    )
    blank_ghost = jnp.zeros((6, 4, slot_count, 128), jnp.float32)
    stacked_rows = with_halo(block_data, (("vt", 1),), 1)
    below_rows = shifted(stacked_rows, "ax", 1)
    above_rows = shifted(stacked_rows, "ax", -1)
    joined = jnp.concatenate([below_rows, stacked_rows, above_rows], axis=2)
    ghost_blocks = pick_blocks(blank_ghost, joined, my_layer - 1, my_axial - 1, 3, neighbour_at)
    flux_liquid = jnp.zeros_like(liquid)
    flux_hydrate = jnp.zeros_like(liquid)
    for direction in range(6):
        along = direction // 2
        other = ghost_blocks[direction]
        near_liquid = across(liquid, other[0], direction)
        near_hydrate = across(hydrate, other[1], direction)
        near_speed = across(velocity[along], other[2], direction)
        near_live = across(live_cells, other[3], direction)
        outward_sign = 1.0 if direction % 2 == 1 else -1.0
        weight = live_cells * near_live
        flux_liquid = flux_liquid + face_flux(
            liquid, near_liquid, velocity[along], near_speed, weight, outward_sign
        )
        flux_hydrate = flux_hydrate + face_flux(
            hydrate, near_hydrate, velocity[along], near_speed, weight, outward_sign
        )
    rate_cell = jnp.zeros_like(liquid)
    for phase_kind in range(growth_rates.shape[0]):
        rate_cell = rate_cell + jnp.where(phase_ids[0] == phase_kind, growth_rates[phase_kind], 0.0)
    growth = rate_cell * arrived[5] * liquid * (1.0 - hydrate)
    liquid_next = live_cells * (liquid - time_step * flux_liquid - time_step * growth)
    hydrate_next = live_cells * (hydrate - time_step * flux_hydrate + time_step * growth)
    fractions_out = jnp.stack([liquid_next, hydrate_next])[:, None]
    motion_out = (arrived[2:] * live_cells[None])[:, None]
    return (fractions_out, motion_out)


def solution(mesh):
    in_specs = (
        P(None, "vt", "ax", None),
        P(None, "vt", "ax", None),
        P("vt", "ax"),
        P("vt", "ax"),
        P(None, "vt", "ax"),
        P("vt", "ax", None),
        P(),
    )
    out_specs = (P(None, "vt", "ax", None), P(None, "vt", "ax", None))
    return jax.shard_map(
        on_device, mesh=mesh, in_specs=in_specs, out_specs=out_specs, check_vma=False
    )
```

profile of v0, /device:TPU:1, one launch (start us, length us, event | category | flops | bytes accessed | tf_op | source)
XLA Modules:
  0.0 310.9 jit_solution(15104517045077024319)
XLA Ops:
  2.8 1.5 pad_maximum_fusion.2
  5.9 2.0 collective-permute-start
  9.5 4.5 %collective-permute-start.1 = (f32[6,16,128]{2,0,1:T(8,128)}, f32[6,16,128]{2,0,1:T(8,128)S(1)}, u32[]{:S(2)}, u32[]{:S(2)}) collective-permute-start(f32[6,16,128]{2,0,1:T(8,128)} %bitcast_select_fusion.1), channel_id=1, source_target_pairs={{0,4},{4,8},{8,12},{12,16},{16,20},{20,24},{24,28},{1,5},{5,9},{9,... | collective-permute-start | bytes 147464 | tf_op jit(solution)/shard_map/ppermute | solution.py:17
  25.6 1.9 gather_fusion.1
  27.6 3.0 gather_fusion.3
  30.6 2.7 fusion
  33.4 1.0 copy-done.42
  34.6 3.3 %collective-permute-start.2 = (f32[6,1,512,128]{3,2,1,0:T(8,128)S(1)}, f32[6,1,512,128]{3,2,1,0:T(8,128)S(1)}, u32[]{:S(2)}, u32[]{:S(2)}) collective-permute-start(f32[6,1,512,128]{3,2,1,0:T(8,128)S(1)} %get-tuple-element.59), channel_id=1, source_target_pairs={{0,1},{1,2},{2,3},{4,5},{5,6},{6,7},{8,9},{9,10},{10,11},{12,13},{... | collective-permute-start | bytes 4718600 | tf_op jit(solution)/shard_map/ppermute | solution.py:27
  37.9 1.3 collective-permute-start.3
  44.5 27.5 %collective-permute-done.2 = f32[6,1,512,128]{3,2,1,0:T(8,128)S(1)} collective-permute-done((f32[6,1,512,128]{3,2,1,0:T(8,128)S(1)}, f32[6,1,512,128]{3,2,1,0:T(8,128)S(1)}, u32[]{:S(2)}, u32[]{:S(2)}) %collective-permute-start.2) | collective-permute-done | bytes 1572896 | tf_op jit(solution)/shard_map/ppermute | solution.py:27
  71.9 4.1 %collective-permute-done.3 = f32[6,1,512,128]{3,2,1,0:T(8,128)S(1)} collective-permute-done((f32[6,1,512,128]{3,2,1,0:T(8,128)S(1)}, f32[6,1,512,128]{3,2,1,0:T(8,128)S(1)}, u32[]{:S(2)}, u32[]{:S(2)}) %collective-permute-start.3) | collective-permute-done | bytes 1572896 | tf_op jit(solution)/shard_map/ppermute | solution.py:28
  76.7 3.0 collective-permute-start.4
  79.8 1.9 collective-permute-start.5
  97.4 1.0 fusion.3
  98.5 32.3 %collective-permute-done.4 = f32[6,3,512,128]{3,2,1,0:T(8,128)S(1)} collective-permute-done((f32[6,3,512,128]{3,2,1,0:T(8,128)S(1)}, f32[6,3,512,128]{3,2,1,0:T(8,128)S(1)}, u32[]{:S(2)}, u32[]{:S(2)}) %collective-permute-start.4) | collective-permute-done | bytes 4718624 | tf_op jit(solution)/shard_map/ppermute | solution.py:17
  130.8 52.8 %collective-permute-done.5 = f32[6,3,512,128]{3,2,1,0:T(8,128)S(1)} collective-permute-done((f32[6,3,512,128]{3,2,1,0:T(8,128)S(1)}, f32[6,3,512,128]{3,2,1,0:T(8,128)S(1)}, u32[]{:S(2)}, u32[]{:S(2)}) %collective-permute-start.5) | collective-permute-done | bytes 4718624 | tf_op jit(solution)/shard_map/ppermute | solution.py:17
  183.5 5.3 %pad_maximum_fusion = f32[6,3,1536,128]{3,2,0,1:T(8,128)} fusion(f32[6,1,512,128]{3,2,0,1:T(8,128)S(1)} %bitcast.444, f32[6,1,512,128]{3,2,0,1:T(8,128)S(1)} %get-tuple-element.58, f32[6,1,512,128]{3,2,0,1:T(8,128)S(1)} %bitcast.442, f32[6,3,512,128]{3,2,1,0:T(8,128)S(1)} %collective-permute-done.4, f32[6,3,512,128]{3,2,1,0:T(8,128)S(1)} %collective-permute-done.5), kind=kLoop, calls=%fused_computation.28 | loop fusion | flops 14155776 | bytes 28311552 | tf_op jit(solution)/shard_map/concatenate | solution.py:134
  188.9 9.7 %fusion.125 = (f32[1,3,1536,128]{3,2,0,1:T(8,128)}, f32[1,3,1536,128]{3,2,0,1:T(8,128)}, f32[1,3,1536,128]{3,2,0,1:T(8,128)}, f32[1,3,1536,128]{3,2,0,1:T(8,128)...) fusion(f32[6,3,1536,128]{3,2,0,1:T(8,128)} %pad_maximum_fusion), kind=kLoop, calls=%fused_computation.447 | loop fusion | bytes 28311552 | tf_op jit(solution)/shard_map/slice | solution.py:87
  198.6 1.0 gather_fusion.24
  199.6 2.7 gather_fusion.25
  202.3 2.7 gather_fusion.26
  205.0 2.7 gather_fusion.27
  212.9 1.0 gather_fusion.20
  213.9 2.7 gather_fusion.21
  216.6 2.7 gather_fusion.22
  219.3 3.3 %gather_fusion.23 = f32[512,128]{1,0:T(8,128)} fusion(f32[4608,128]{1,0:T(8,128)} %bitcast.424, s32[1024]{0:T(1024)S(1)} %copy-done.45), kind=kCustom, calls=%fused_computation.23.clone | custom fusion | bytes 526336 | tf_op jit(solution)/shard_map/jit(_take)/gather | solution.py:87
  222.7 1.1 select_bitcast_fusion.7
  228.7 1.0 gather_fusion.16
  229.8 2.7 gather_fusion.17
  232.5 3.3 %gather_fusion.19 = f32[512,128]{1,0:T(8,128)} fusion(f32[4608,128]{1,0:T(8,128)} %bitcast.425, s32[1024]{0:T(1024)S(1)} %pad_clamp_fusion.2), kind=kCustom, calls=%fused_computation.19.clone | custom fusion | bytes 526336 | tf_op jit(solution)/shard_map/jit(_take)/gather | solution.py:87
  235.8 3.3 %gather_fusion.18 = f32[512,128]{1,0:T(8,128)} fusion(f32[4608,128]{1,0:T(8,128)} %bitcast.437, s32[1024]{0:T(1024)S(1)} %pad_clamp_fusion.2), kind=kCustom, calls=%fused_computation.18.clone | custom fusion | bytes 526336 | tf_op jit(solution)/shard_map/jit(_take)/gather | solution.py:87
  239.1 1.2 select_bitcast_fusion.11
  246.3 3.3 %gather_fusion.13 = f32[512,128]{1,0:T(8,128)} fusion(f32[4608,128]{1,0:T(8,128)} %bitcast.432, s32[1024]{0:T(1024)S(1)} %pad_clamp_fusion.3), kind=kCustom, calls=%fused_computation.13.clone | custom fusion | bytes 526336 | tf_op jit(solution)/shard_map/jit(_take)/gather | solution.py:87
  249.6 3.3 %gather_fusion.14 = f32[512,128]{1,0:T(8,128)} fusion(f32[4608,128]{1,0:T(8,128)} %bitcast.438, s32[1024]{0:T(1024)S(1)} %pad_clamp_fusion.3), kind=kCustom, calls=%fused_computation.14.clone | custom fusion | bytes 526336 | tf_op jit(solution)/shard_map/jit(_take)/gather | solution.py:87
  252.9 3.3 %gather_fusion.15 = f32[512,128]{1,0:T(8,128)} fusion(f32[4608,128]{1,0:T(8,128)} %bitcast.426, s32[1024]{0:T(1024)S(1)} %pad_clamp_fusion.3), kind=kCustom, calls=%fused_computation.15.clone | custom fusion | bytes 526336 | tf_op jit(solution)/shard_map/jit(_take)/gather | solution.py:87
  256.2 1.2 select_bitcast_fusion.15
  262.4 1.6 gather_fusion.8
  264.1 3.3 %gather_fusion.9 = f32[512,128]{1,0:T(8,128)} fusion(f32[4608,128]{1,0:T(8,128)} %bitcast.433, s32[1024]{0:T(1024)S(1)} %pad_clamp_fusion.4), kind=kCustom, calls=%fused_computation.9.clone | custom fusion | bytes 526336 | tf_op jit(solution)/shard_map/jit(_take)/gather | solution.py:87
  267.4 3.3 %gather_fusion.11 = f32[512,128]{1,0:T(8,128)} fusion(f32[4608,128]{1,0:T(8,128)} %bitcast.427, s32[1024]{0:T(1024)S(1)} %pad_clamp_fusion.4), kind=kCustom, calls=%fused_computation.11.clone | custom fusion | bytes 526336 | tf_op jit(solution)/shard_map/jit(_take)/gather | solution.py:87
  270.7 3.3 %gather_fusion.10 = f32[512,128]{1,0:T(8,128)} fusion(f32[4608,128]{1,0:T(8,128)} %bitcast.435, s32[1024]{0:T(1024)S(1)} %pad_clamp_fusion.4), kind=kCustom, calls=%fused_computation.10.clone | custom fusion | bytes 526336 | tf_op jit(solution)/shard_map/jit(_take)/gather | solution.py:87
  274.0 1.3 select_bitcast_fusion.19
  280.9 3.3 %gather_fusion.5 = f32[512,128]{1,0:T(8,128)} fusion(f32[4608,128]{1,0:T(8,128)} %bitcast.434, s32[1024]{0:T(1024)S(1)} %pad_clamp_fusion.5), kind=kCustom, calls=%fused_computation.5.clone | custom fusion | bytes 526336 | tf_op jit(solution)/shard_map/jit(_take)/gather | solution.py:87
  284.2 3.3 %gather_fusion.6 = f32[512,128]{1,0:T(8,128)} fusion(f32[4608,128]{1,0:T(8,128)} %bitcast.436, s32[1024]{0:T(1024)S(1)} %pad_clamp_fusion.5), kind=kCustom, calls=%fused_computation.6.clone | custom fusion | bytes 526336 | tf_op jit(solution)/shard_map/jit(_take)/gather | solution.py:87
  287.5 3.3 %gather_fusion.7 = f32[512,128]{1,0:T(8,128)} fusion(f32[4608,128]{1,0:T(8,128)} %bitcast.428, s32[1024]{0:T(1024)S(1)} %pad_clamp_fusion.5), kind=kCustom, calls=%fused_computation.7.clone | custom fusion | bytes 526336 | tf_op jit(solution)/shard_map/jit(_take)/gather | solution.py:87
  290.8 1.6 gather_fusion.4
  292.4 1.3 select_bitcast_fusion.23
  298.4 8.7 %fusion.21 = (f32[1,512,128]{2,1,0:T(8,128)S(1)}, f32[1,512,128]{2,1,0:T(8,128)S(1)}, f32[1,512,128]{2,1,0:T(8,128)S(1)}, f32[1,512,128]{2,1,0:T(8,128)S(1)}, f3...) fusion(f32[1,512,7]{2,1,0:T(8,128)S(1)} %slice_bitcast_fusion.1, ...), kind=kLoop, calls=%fused_computation.192 | loop fusion | flops 8781824 | bytes 14945040 | tf_op jit(solution)/shard_map/mul | solution.py:157
  307.1 2.9 fusion.63
  (288 shorter events, 70.2 us)
Async XLA Ops:
  4.2 9.7 %copy-start.47 = (s32[1,512]{1,0:T(1,128)S(1)}, s32[1,512]{1,0:T(1,128)}, u32[]{:S(2)}) copy-start(s32[1,512]{1,0:T(1,128)} %param.15) | copy-start | bytes 6148
  4.3 10.2 %copy-start.44 = (s32[6,1,512]{2,1,0:T(1,128)S(1)}, s32[6,1,512]{2,1,0:T(1,128)}, u32[]{:S(2)}) copy-start(s32[6,1,512]{2,1,0:T(1,128)} %param.17) | copy-start | bytes 36868
  4.3 13.8 %copy-start.48 = (s32[1,512]{1,0:T(1,128)S(1)}, s32[1,512]{1,0:T(1,128)}, u32[]{:S(2)}) copy-start(s32[1,512]{1,0:T(1,128)} %param.16) | copy-start | bytes 6148
  4.3 20.1 %copy-start.49 = (f32[4]{0:T(128)S(1)}, f32[4]{0:T(128)}, u32[]{:S(2)}) copy-start(f32[4]{0:T(128)} %param.19) | copy-start | bytes 52
  5.9 19.7 %collective-permute-start = (f32[6,16,128]{2,0,1:T(8,128)S(1)}, f32[6,16,128]{2,0,1:T(8,128)S(1)}, u32[]{:S(2)}, u32[]{:S(2)}) collective-permute-start(f32[6,16,128]{2,0,1:T(8,128)S(1)} %bitcast_select_fusion.2), channel_id=1, source_target_pairs={{4,0},{8,4},{12,8},{16,12},{20,16},{24,20},{28,24},{5,1},{9,5},{13... | collective-permute-start | bytes 147464 | tf_op jit(solution)/shard_map/ppermute | solution.py:17
  9.5 18.1 %collective-permute-start.1 = (f32[6,16,128]{2,0,1:T(8,128)}, f32[6,16,128]{2,0,1:T(8,128)S(1)}, u32[]{:S(2)}, u32[]{:S(2)}) collective-permute-start(f32[6,16,128]{2,0,1:T(8,128)} %bitcast_select_fusion.1), channel_id=1, source_target_pairs={{0,4},{4,8},{8,12},{12,16},{16,20},{20,24},{24,28},{1,5},{5,9},{9,... | collective-permute-start | bytes 147464 | tf_op jit(solution)/shard_map/ppermute | solution.py:17
  27.5 3.0 copy-start.2
  27.5 3.0 copy-start.62
  27.5 3.0 copy-start.63
  27.5 3.0 copy-start.64
  27.6 3.0 copy-start.65
  33.3 64.2 %copy-start = (f32[6,512,128]{2,1,0:T(8,128)}, f32[6,512,128]{2,1,0:T(8,128)S(1)}, u32[]{:S(2)}) copy-start(f32[6,512,128]{2,1,0:T(8,128)S(1)} %fusion) | copy-start | bytes 4718596
  34.6 37.3 %collective-permute-start.2 = (f32[6,1,512,128]{3,2,1,0:T(8,128)S(1)}, f32[6,1,512,128]{3,2,1,0:T(8,128)S(1)}, u32[]{:S(2)}, u32[]{:S(2)}) collective-permute-start(f32[6,1,512,128]{3,2,1,0:T(8,128)S(1)} %get-tuple-element.59), channel_id=1, source_target_pairs={{0,1},{1,2},{2,3},{4,5},{5,6},{6,7},{8,9},{9,10},{10,11},{12,13},{... | collective-permute-start | bytes 4718600 | tf_op jit(solution)/shard_map/ppermute | solution.py:27
  37.9 38.2 %collective-permute-start.3 = (f32[6,1,512,128]{3,2,1,0:T(8,128)S(1)}, f32[6,1,512,128]{3,2,1,0:T(8,128)S(1)}, u32[]{:S(2)}, u32[]{:S(2)}) collective-permute-start(f32[6,1,512,128]{3,2,1,0:T(8,128)S(1)} %get-tuple-element.59), channel_id=1, source_target_pairs={{1,0},{2,1},{3,2},{5,4},{6,5},{7,6},{9,8},{10,9},{11,10},{13,12},{... | collective-permute-start | bytes 4718600 | tf_op jit(solution)/shard_map/ppermute | solution.py:28
  76.7 54.1 %collective-permute-start.4 = (f32[6,3,512,128]{3,2,1,0:T(8,128)S(1)}, f32[6,3,512,128]{3,2,1,0:T(8,128)S(1)}, u32[]{:S(2)}, u32[]{:S(2)}) collective-permute-start(f32[6,3,512,128]{3,2,1,0:T(8,128)S(1)} %copy.222), channel_id=1, source_target_pairs={{0,4},{4,8},{8,12},{12,16},{16,20},{20,24},{24,28},{1,5},{5,9},{9,... | collective-permute-start | bytes 14155784 | tf_op jit(solution)/shard_map/ppermute | solution.py:17
  79.8 103.8 %collective-permute-start.5 = (f32[6,3,512,128]{3,2,1,0:T(8,128)S(1)}, f32[6,3,512,128]{3,2,1,0:T(8,128)S(1)}, u32[]{:S(2)}, u32[]{:S(2)}) collective-permute-start(f32[6,3,512,128]{3,2,1,0:T(8,128)S(1)} %copy.222), channel_id=1, source_target_pairs={{4,0},{8,4},{12,8},{16,12},{20,16},{24,20},{28,24},{5,1},{9,5},{13... | collective-permute-start | bytes 14155784 | tf_op jit(solution)/shard_map/ppermute | solution.py:17
  188.9 9.7 %copy-start.46 = (s32[1024]{0:T(1024)S(1)}, s32[1024]{0:T(1024)}, u32[]{:S(2)}) copy-start(s32[1024]{0:T(1024)} %pad_clamp_fusion) | copy-start | bytes 12292
  202.3 5.4 %copy-start.59 = (pred[512]{0:T(512)(128)(4,1)S(1)}, pred[512]{0:T(512)(128)(4,1)}, u32[]{:S(2)}) copy-start(pred[512]{0:T(512)(128)(4,1)} %compare_and_fusion.2) | copy-start | bytes 1540
  205.0 2.9 copy-start.61
  208.0 4.8 %copy-start.45 = (s32[1024]{0:T(1024)S(1)}, s32[1024]{0:T(1024)}, u32[]{:S(2)}) copy-start(s32[1024]{0:T(1024)} %pad_clamp_fusion.1) | copy-start | bytes 12292
  216.6 6.0 %copy-start.57 = (pred[512]{0:T(512)(128)(4,1)S(1)}, pred[512]{0:T(512)(128)(4,1)}, u32[]{:S(2)}) copy-start(pred[512]{0:T(512)(128)(4,1)} %compare_and_fusion.3) | copy-start | bytes 1540
  219.3 4.4 %copy-start.60 = (pred[512]{0:T(512)(128)(4,1)S(1)}, pred[512]{0:T(512)(128)(4,1)}, u32[]{:S(2)}) copy-start(pred[512]{0:T(512)(128)(4,1)} %get-tuple-element.16) | copy-start | bytes 1540
  232.5 6.6 %copy-start.55 = (pred[512]{0:T(512)(128)(4,1)S(1)}, pred[512]{0:T(512)(128)(4,1)}, u32[]{:S(2)}) copy-start(pred[512]{0:T(512)(128)(4,1)} %compare_and_fusion.4) | copy-start | bytes 1540
  235.8 4.5 %copy-start.58 = (pred[512]{0:T(512)(128)(4,1)S(1)}, pred[512]{0:T(512)(128)(4,1)}, u32[]{:S(2)}) copy-start(pred[512]{0:T(512)(128)(4,1)} %get-tuple-element.17) | copy-start | bytes 1540
  249.6 6.6 %copy-start.53 = (pred[512]{0:T(512)(128)(4,1)S(1)}, pred[512]{0:T(512)(128)(4,1)}, u32[]{:S(2)}) copy-start(pred[512]{0:T(512)(128)(4,1)} %compare_and_fusion.5) | copy-start | bytes 1540
  252.9 4.6 %copy-start.56 = (pred[512]{0:T(512)(128)(4,1)S(1)}, pred[512]{0:T(512)(128)(4,1)}, u32[]{:S(2)}) copy-start(pred[512]{0:T(512)(128)(4,1)} %get-tuple-element.18) | copy-start | bytes 1540
  267.4 6.6 %copy-start.51 = (pred[512]{0:T(512)(128)(4,1)S(1)}, pred[512]{0:T(512)(128)(4,1)}, u32[]{:S(2)}) copy-start(pred[512]{0:T(512)(128)(4,1)} %compare_and_fusion.6) | copy-start | bytes 1540
  270.7 4.6 %copy-start.54 = (pred[512]{0:T(512)(128)(4,1)S(1)}, pred[512]{0:T(512)(128)(4,1)}, u32[]{:S(2)}) copy-start(pred[512]{0:T(512)(128)(4,1)} %get-tuple-element.19) | copy-start | bytes 1540
  287.5 4.9 %copy-start.50 = (pred[512]{0:T(512)(128)(4,1)S(1)}, pred[512]{0:T(512)(128)(4,1)}, u32[]{:S(2)}) copy-start(pred[512]{0:T(512)(128)(4,1)} %compare_and_fusion.7) | copy-start | bytes 1540
  290.8 3.0 copy-start.52
  293.8 2.3 copy-start.41
  293.9 2.2 copy-start.33
  294.0 2.2 copy-start.34
  294.0 2.2 copy-start.35
  294.9 2.6 copy-start.1
  295.0 2.6 copy-start.4
  295.0 2.7 copy-start.5
  295.0 2.7 copy-start.6
  295.0 2.8 copy-start.7
  295.0 2.9 copy-start.8
  295.0 2.9 copy-start.9
  295.0 3.0 copy-start.10
  295.0 3.0 copy-start.11
  295.0 3.1 %copy-start.12 = (f32[1,512,24]{2,1,0:T(8,128)S(1)}, f32[1,512,24]{2,1,0:T(8,128)}, u32[]{:S(2)}) copy-start(f32[1,512,24]{2,1,0:T(8,128)} %slice_bitcast_fusion.52) | copy-start | bytes 147460
  295.0 3.2 %copy-start.13 = (f32[1,512,104]{2,1,0:T(8,128)S(1)}, f32[1,512,104]{2,1,0:T(8,128)}, u32[]{:S(2)}) copy-start(f32[1,512,104]{2,1,0:T(8,128)} %slice_bitcast_fusion.53) | copy-start | bytes 638980
  295.1 3.2 %copy-start.14 = (f32[1,512,24]{2,1,0:T(8,128)S(1)}, f32[1,512,24]{2,1,0:T(8,128)}, u32[]{:S(2)}) copy-start(f32[1,512,24]{2,1,0:T(8,128)} %slice_bitcast_fusion.57) | copy-start | bytes 147460
  295.1 3.3 %copy-start.15 = (f32[1,512,104]{2,1,0:T(8,128)S(1)}, f32[1,512,104]{2,1,0:T(8,128)}, u32[]{:S(2)}) copy-start(f32[1,512,104]{2,1,0:T(8,128)} %slice_bitcast_fusion.58) | copy-start | bytes 638980
  298.4 8.7 %copy-start.43 = (f32[1,512,120]{2,1,0:T(8,128)S(1)}, f32[1,512,120]{2,1,0:T(8,128)}, u32[]{:S(2)}) copy-start(f32[1,512,120]{2,1,0:T(8,128)} %get-tuple-element.84) | copy-start | bytes 737284
  (24 other events, 47.3 us)
where the time goes:
time: 312 us; the launch traced here: 311 us
  local copies, waits for them, and re-layouts  132 us (42%)
  waiting for transfers between devices  117 us (38%)
  other arithmetic  43.7 us (14%)
  starting transfers between devices  15.9 us (5%)
    ppermute x4, waiting for transfers between devices, shifted(): lax.ppermute(value, axis, [(source, source + steps) for source in range(f...  85.1 us
    gather x24, local copies, waits for them, and re-layouts, pick_blocks(): jnp.take(flattened[member], picked, axis=0)  63.2 us
    ppermute x1, waiting for transfers between devices, with_halo(): before = lax.ppermute(last, axis, up)  27.5 us
    concatenate x18, local copies, waits for them, and re-layouts, across(): inside = jnp.roll(own, -stride, axis=-1)  15.6 us
    concatenate x24, local copies, waits for them, and re-layouts, across(): from_other = jnp.roll(other, (extent - 1) * stride, axis=-1)  14.5 us
    ppermute x4, starting transfers between devices, shifted(): lax.ppermute(value, axis, [(source, source + steps) for source in range(f...  11.3 us
    concatenate x24, local copies, waits for them, and re-layouts, across(): from_other = jnp.roll(other, -(extent - 1) * stride, axis=-1)  10.3 us
    slice x1, local copies, waits for them, and re-layouts, pick_blocks(): flattened[member]  9.69 us
  transfers between devices with their start and end apart: 6, of which 4 were waited for; matrix products, arithmetic and copies ran while one was open for 12% of the time, Pallas kernels for 0%

commit v1 on v0

v1 whole, which is shorter than its diff:
```python
import functools

import jax
import jax.numpy as jnp
from jax import lax
from jax.experimental import pallas as pl
from jax.experimental.pallas import tpu as pltpu
from jax.sharding import PartitionSpec as P

MOVES = 16
SPAN = 64
CELLS = 128
MESH = pl.DeviceIdType.MESH
HIGH = lax.Precision.HIGHEST
F32 = jnp.float32
BF16 = jnp.bfloat16

axis_stride = (1, 32, 8)
axis_extent = (8, 4, 4)
time_step = 0.25
table_of = (0, 0, 1, 2, 3, 4)
PACK = SPAN + MOVES
ROWS_AX = 5 * PACK + 8
ROWS_MV = 6 * MOVES + 8


def place_of(direction, member):
    return member + (4 if direction == 1 else 0)


def roll_lanes(x, shift):
    shift = shift % CELLS
    return x if shift == 0 else pltpu.roll(x, shift, 1)


def coordinates(rows):
    lane = lax.broadcasted_iota(jnp.int32, (rows, CELLS), 1)
    return (lane & 7, (lane >> 5) & 3, (lane >> 3) & 3)


def halves(x):
    hi = x.astype(BF16)
    return hi, (x - hi.astype(F32)).astype(BF16)


def kernel(na, nv, frac, mot, home, cnt, nb, phase, rates, fout, mout,
           cells, mv_send, mv_recv, mv_pay, tab, ax_send, ax_recv, vt_recv, win, acc, rowbuf, cols,
           mv_ss, mv_rs, ax_ss, ax_rs, vt_ss, vt_rs):
    slots = frac.shape[1]
    shift = slots.bit_length() - 1
    total = slots * na
    ax, vt = lax.axis_index("ax"), lax.axis_index("vt")

    def inside(a, v):
        return (a >= 0) & (a < na) & (v >= 0) & (v < nv)

    barrier = pltpu.get_barrier_semaphore()
    others = [(i, j) for i in (-1, 0, 1) for j in (-1, 0, 1) if (i, j) != (0, 0)]
    greeted = 0
    for i, j in others:
        there = inside(ax + i, vt + j)
        greeted = greeted + there.astype(jnp.int32)

        @pl.when(there)
        def _():
            pl.semaphore_signal(barrier, inc=1, device_id=(ax + i, vt + j), device_id_type=MESH)

    steps = (1, -1)

    def mover(s, peer):
        return pltpu.make_async_remote_copy(
            src_ref=mv_send.at[s], dst_ref=mv_recv.at[s], send_sem=mv_ss.at[s], recv_sem=mv_rs.at[s],
            device_id=peer, device_id_type=MESH)

    def axial(s, v, peer):
        return pltpu.make_async_remote_copy(
            src_ref=ax_send.at[s], dst_ref=ax_recv.at[s * 3 + v], send_sem=ax_ss.at[s * 3 + v],
            recv_sem=ax_rs.at[s * 3 + v], device_id=peer, device_id_type=MESH)

    def vertical(s, t, peer):
        return pltpu.make_async_remote_copy(
            src_ref=tab.at[t], dst_ref=vt_recv.at[s * 5 + t], send_sem=vt_ss.at[s * 5 + t],
            recv_sem=vt_rs.at[s * 5 + t], device_id=peer, device_id_type=MESH)

    slot_row = lax.broadcasted_iota(jnp.int32, (1, slots), 1)
    target = home[...]
    target_ax = (target >> shift) & (na - 1)
    linked = nb[...]
    linked_ax = jnp.where(linked >= 0, (linked >> shift) & (na - 1), -5)
    masks = [(target_ax == ax + 1), (target_ax == ax - 1)]
    reach_up = jnp.max((linked_ax == ax + 1).astype(jnp.int32), axis=0, keepdims=True) > 0
    reach_down = jnp.max((linked_ax == ax - 1).astype(jnp.int32), axis=0, keepdims=True) > 0
    masks += [reach_up & (slot_row < slots - SPAN), reach_down & (slot_row >= SPAN)]
    masks = [m.astype(F32) for m in masks]
    mask8 = jnp.concatenate(masks + [jnp.zeros((4, slots), F32)], axis=0)
    before = lax.broadcasted_iota(jnp.int32, (slots, slots), 0) < lax.broadcasted_iota(jnp.int32, (slots, slots), 1)
    rank = jnp.dot(mask8.astype(BF16), before.astype(F32).astype(BF16), preferred_element_type=F32)
    rank = jnp.where(mask8 > 0.0, rank, -1.0)

    rowbuf[...] = jnp.concatenate(
        [linked.astype(F32), cnt[...].astype(F32), jnp.zeros((1, slots), F32)], axis=0)
    cols[...] = rowbuf[...].T

    def one_hot(which, rows):
        m = (lax.broadcasted_iota(jnp.int32, (rows, slots), 0) & (MOVES - 1)).astype(F32)
        return (rank[which:which + 1] == m).astype(F32)

    def names(which, row):
        return lax.dot_general(
            jnp.broadcast_to(row, (8, slots)), one_hot(which, CELLS), (((1,), (1,)), ((), ())),
            precision=HIGH, preferred_element_type=F32)

    target_slot = (target & (slots - 1)).astype(F32) + 1.0
    global_row = (slot_row + (vt * total + ax * slots)).astype(F32) + 1.0
    pick = jnp.concatenate([one_hot(0, MOVES), one_hot(1, MOVES)], axis=0)
    for f in range(6):
        source = frac[f] if f < 2 else mot[f - 2]
        packed = jnp.dot(pick, source, precision=HIGH, preferred_element_type=F32)
        for s in range(2):
            mv_send[s, f * MOVES:(f + 1) * MOVES] = packed[s * MOVES:(s + 1) * MOVES]
    for s in range(2):
        mv_send[s, 6 * MOVES:] = names(s, target_slot)
        ax_send[s, 5 * PACK:] = names(2 + s, global_row)

    for s in range(2):
        @pl.when(jnp.logical_not(inside(ax - steps[s], vt)))
        def _():
            mv_recv[s] = jnp.zeros((ROWS_MV, CELLS), F32)

        @pl.when(jnp.logical_not(inside(ax, vt - steps[s])))
        def _():
            for t in range(5):
                vt_recv[s * 5 + t] = jnp.zeros((slots, CELLS), F32)

        for v in range(3):
            @pl.when(jnp.logical_not(inside(ax - steps[s], vt - (v - 1))))
            def _():
                ax_recv[s * 3 + v] = jnp.zeros((ROWS_AX, CELLS), F32)

    pl.semaphore_wait(barrier, greeted)
    for s in range(2):
        @pl.when(inside(ax + steps[s], vt))
        def _():
            mover(s, (ax + steps[s], vt)).start()

    mv_pay[...] = jnp.zeros_like(mv_pay)
    for s in range(2):
        @pl.when(inside(ax - steps[s], vt))
        def _():
            mover(s, (ax - steps[s], vt)).wait_recv()

    lane1 = lax.broadcasted_iota(jnp.int32, (1, CELLS), 1)
    arrivals = jnp.where(lane1 < MOVES, mv_recv[0, 6 * MOVES:6 * MOVES + 1],
                         jnp.where(lane1 < 2 * MOVES, mv_recv[1, 6 * MOVES:6 * MOVES + 1], 0.0)) - 1.0
    for f in range(6):
        for s in range(2):
            mv_pay[f, s * MOVES:(s + 1) * MOVES] = mv_recv[s, f * MOVES:(f + 1) * MOVES]

    chunk = 64

    @pl.loop(0, slots // chunk)
    def _(c):
        start = pl.multiple_of(c * chunk, chunk)
        rows = pl.ds(start, chunk)
        at = (lax.broadcasted_iota(jnp.int32, (chunk, CELLS), 0) + start).astype(F32)
        select = (at == arrivals).astype(F32)
        hit = jnp.max(select, axis=1, keepdims=True) > 0.0
        lane = lax.broadcasted_iota(jnp.int32, (chunk, CELLS), 1)
        live = (lane.astype(F32) < cols[rows, 6:7]).astype(F32)
        now = []
        for f in range(6):
            old = frac[f, rows] if f < 2 else mot[f - 2, rows]
            came = jnp.dot(select, mv_pay[f], precision=HIGH, preferred_element_type=F32)
            value = jnp.where(hit, came, old)
            cells[f, rows] = value
            now.append(value)
            if f >= 2:
                mout[f - 2, rows] = value * live
        coordinate = coordinates(chunk)
        for t in range(5):
            made = jnp.zeros((chunk, CELLS), F32)
            for d in range(6):
                if table_of[d] != t:
                    continue
                k = d // 2
                edge = axis_extent[k] - 1 if d % 2 == 0 else 0
                for member, value in enumerate((now[0], now[1], now[2 + k], live)):
                    p = place_of(d, member)
                    made = jnp.where(coordinate[k] == p, roll_lanes(value, (p - edge) * axis_stride[k]), made)
            tab[t, rows] = made
            hi, lo = halves(made)
            win[t, rows, :CELLS] = hi
            win[t, rows, CELLS:] = lo

    for t in range(5):
        for s in range(2):
            @pl.when(inside(ax, vt + steps[s]))
            def _():
                vertical(s, t, (ax, vt + steps[s])).start()

    pick = jnp.concatenate([one_hot(2, MOVES), one_hot(3, MOVES)], axis=0).astype(BF16)
    for t in range(5):
        both = jnp.dot(pick, win[t, :slots], preferred_element_type=F32)
        packed = both[:, :CELLS] + both[:, CELLS:]
        for s in range(2):
            first = slots - SPAN if s == 0 else 0
            ax_send[s, t * PACK:t * PACK + SPAN] = tab[t, first:first + SPAN]
            ax_send[s, t * PACK + SPAN:(t + 1) * PACK] = packed[s * MOVES:(s + 1) * MOVES]
    for s in range(2):
        for v in range(3):
            @pl.when(inside(ax + steps[s], vt + v - 1))
            def _():
                axial(s, v, (ax + steps[s], vt + v - 1)).start()

    tall = 128

    def gather(t, keys, fresh):
        @pl.loop(0, slots // tall)
        def _(c):
            rows = pl.ds(pl.multiple_of(c * tall, tall), tall)
            for d in range(6):
                if table_of[d] != t:
                    continue
                match = (cols[rows, d:d + 1] == keys).astype(F32).astype(BF16)
                both = jnp.dot(match, win[t, :slots], preferred_element_type=F32)
                both = both[:, :CELLS] + both[:, CELLS:]
                if fresh:
                    acc[d, rows] = both
                else:
                    acc[d, rows] += both

    for t in range(5):
        gather(t, global_row - 1.0, True)

    for s in range(2):
        for v in range(3):
            @pl.when(inside(ax - steps[s], vt - (v - 1)))
            def _():
                axial(s, v, (ax - steps[s], vt - (v - 1))).wait_recv()
    layer_keys = jnp.full((1, slots), -2.0, F32)
    which = slot_row >> (SPAN.bit_length() - 1)
    within = slot_row & (SPAN - 1)
    for s in range(2):
        for v in range(3):
            w = s * 3 + v
            base = (vt - (v - 1)) * total + (ax - steps[s]) * slots + (slots - SPAN if s == 0 else 0)
            layer_keys = jnp.where(which == w, (within + base).astype(F32), layer_keys)
    other_keys = jnp.full((1, CELLS), -2.0, F32)
    for w in range(6):
        row = ax_recv[w, 5 * PACK:5 * PACK + 1]
        row = jnp.where(row > 0.0, row - 1.0, -2.0)
        other_keys = jnp.where((lane1 >> 4) == w, row, other_keys)
    ax_keys = jnp.concatenate([layer_keys[:, :6 * SPAN], other_keys], axis=1)
    for t in range(5):
        for w in range(6):
            hi, lo = halves(ax_recv[w, t * PACK:t * PACK + SPAN])
            win[t, w * SPAN:(w + 1) * SPAN, :CELLS] = hi
            win[t, w * SPAN:(w + 1) * SPAN, CELLS:] = lo
            first = 6 * SPAN + w * MOVES
            hi, lo = halves(ax_recv[w, t * PACK + SPAN:(t + 1) * PACK])
            win[t, first:first + MOVES, :CELLS] = hi
            win[t, first:first + MOVES, CELLS:] = lo
        win[t, 6 * PACK:] = jnp.zeros((slots - 6 * PACK, 2 * CELLS), BF16)
        gather(t, ax_keys, False)

    for t in range(5):
        for s in range(2):
            @pl.when(inside(ax, vt - steps[s]))
            def _():
                vertical(s, t, (ax, vt - steps[s])).wait_recv()

            @pl.loop(0, slots // tall)
            def _(c):
                rows = pl.ds(pl.multiple_of(c * tall, tall), tall)
                hi, lo = halves(vt_recv[s * 5 + t, rows])
                win[t, rows, :CELLS] = hi
                win[t, rows, CELLS:] = lo

            gather(t, (slot_row + ((vt - steps[s]) * total + ax * slots)).astype(F32), False)

    small = 32

    @pl.loop(0, slots // small)
    def _(c):
        rows = pl.ds(pl.multiple_of(c * small, small), small)
        lane = lax.broadcasted_iota(jnp.int32, (small, CELLS), 1)
        live = (lane.astype(F32) < cols[rows, 6:7]).astype(F32)
        coordinate = coordinates(small)
        liquid, hydrate = cells[0, rows], cells[1, rows]
        flux_l = jnp.zeros((small, CELLS), F32)
        flux_h = jnp.zeros((small, CELLS), F32)
        for d in range(6):
            k = d // 2
            stride, extent = axis_stride[k], axis_extent[k]
            edge = 0 if d % 2 == 0 else extent - 1
            step = stride if d % 2 == 0 else -stride
            got = acc[d, rows]
            speed = cells[2 + k, rows]
            near = [
                jnp.where(coordinate[k] == edge, roll_lanes(got, (edge - place_of(d, m)) * stride), roll_lanes(value, step))
                for m, value in enumerate((liquid, hydrate, speed, live))
            ]
            outward = (1.0 if d % 2 else -1.0) * 0.5 * (speed + near[2])
            weight = live * near[3]
            out, into = weight * jnp.maximum(outward, 0.0), weight * jnp.minimum(outward, 0.0)
            flux_l = flux_l + (out * liquid + into * near[0])
            flux_h = flux_h + (out * hydrate + into * near[1])
        rate = jnp.zeros((small, CELLS), F32)
        kinds = phase[rows]
        for kind in range(rates.shape[0]):
            rate = jnp.where(kinds == kind, rates[kind], rate)
        growth = rate * cells[5, rows] * liquid * (1.0 - hydrate)
        fout[0, rows] = live * (liquid - time_step * flux_l - time_step * growth)
        fout[1, rows] = live * (hydrate - time_step * flux_h + time_step * growth)

    for s in range(2):
        @pl.when(inside(ax + steps[s], vt))
        def _():
            mover(s, (ax + steps[s], vt)).wait_send()

        for v in range(3):
            @pl.when(inside(ax + steps[s], vt + v - 1))
            def _():
                axial(s, v, (ax + steps[s], vt + v - 1)).wait_send()

        for t in range(5):
            @pl.when(inside(ax, vt + steps[s]))
            def _():
                vertical(s, t, (ax, vt + steps[s])).wait_send()


def on_device(fractions, motion_fields, new_home, counts, neighbours, phase_ids, growth_rates):
    na, nv = lax.axis_size("ax"), lax.axis_size("vt")
    slots = fractions.shape[2]
    vmem = pl.BlockSpec(memory_space=pltpu.VMEM)
    fout, mout = pl.pallas_call(
        functools.partial(kernel, na, nv),
        out_shape=(jax.ShapeDtypeStruct((2, slots, CELLS), F32), jax.ShapeDtypeStruct((4, slots, CELLS), F32)),
        in_specs=[vmem] * 6 + [pl.BlockSpec(memory_space=pltpu.SMEM)],
        out_specs=(vmem, vmem),
        scratch_shapes=[
            pltpu.VMEM((6, slots, CELLS), F32),
            pltpu.VMEM((2, ROWS_MV, CELLS), F32),
            pltpu.VMEM((2, ROWS_MV, CELLS), F32),
            pltpu.VMEM((6, CELLS, CELLS), F32),
            pltpu.VMEM((5, slots, CELLS), F32),
            pltpu.VMEM((2, ROWS_AX, CELLS), F32),
            pltpu.VMEM((6, ROWS_AX, CELLS), F32),
            pltpu.VMEM((10, slots, CELLS), F32),
            pltpu.VMEM((5, slots, 2 * CELLS), BF16),
            pltpu.VMEM((6, slots, CELLS), F32),
            pltpu.VMEM((8, slots), F32),
            pltpu.VMEM((slots, 8), F32),
            pltpu.SemaphoreType.DMA((2,)),
            pltpu.SemaphoreType.DMA((2,)),
            pltpu.SemaphoreType.DMA((6,)),
            pltpu.SemaphoreType.DMA((6,)),
            pltpu.SemaphoreType.DMA((10,)),
            pltpu.SemaphoreType.DMA((10,)),
        ],
        compiler_params=pltpu.CompilerParams(
            collective_id=0, has_side_effects=True, vmem_limit_bytes=40 * 1024 * 1024),
    )(fractions[:, 0], motion_fields[:, 0], new_home, counts, neighbours[:, 0], phase_ids[0], growth_rates)
    return fout[:, None], mout[:, None]


def solution(mesh):
    in_specs = (
        P(None, "vt", "ax", None),
        P(None, "vt", "ax", None),
        P("vt", "ax"),
        P("vt", "ax"),
        P(None, "vt", "ax"),
        P("vt", "ax", None),
        P(),
    )
    out_specs = (P(None, "vt", "ax", None), P(None, "vt", "ax", None))
    return jax.shard_map(
        on_device, mesh=mesh, in_specs=in_specs, out_specs=out_specs, check_vma=False
    )
```

time: 312 us -> 78.3 us (0.25)
  local copies, waits for them, and re-layouts: 132 us -> 6.36 us
  waiting for transfers between devices: 117 us -> 0 us
  Pallas kernels: 0 us -> 70.3 us
  other arithmetic: 43.7 us -> 0 us
  starting transfers between devices: 15.9 us -> 0 us
    ppermute x6 -> x0, waiting for transfers between devices: 117 us -> none  [the longest x4 85.1 us: shifted(): lax.ppermute(value, axis, [(source, source + steps) for source in range(f...]
    pallas_call x0 -> x1, Pallas kernels: none -> 70.3 us  [on_device(): pl.pallas_call(functools.partial(kernel, na, nv), out_shape=(jax.ShapeDty...]
    gather x28 -> x0, local copies, waits for them, and re-layouts: 69.2 us -> none  [the longest x24 63.2 us: pick_blocks(): jnp.take(flattened[member], picked, axis=0)]
    concatenate x74 -> x0, local copies, waits for them, and re-layouts: 47 us -> none  [the longest x18 15.6 us: across(): inside = jnp.roll(own, -stride, axis=-1)]
    ppermute x6 -> x0, starting transfers between devices: 15.9 us -> none  [the longest x4 11.3 us: shifted(): lax.ppermute(value, axis, [(source, source + steps) for source in range(f...]
    mul x2 -> x0, other arithmetic: 11.6 us -> none  [the longest x1 8.71 us: on_device(): live_cells * (liquid - time_step * flux_liquid - time_step * growth)]
    slice x5 -> x0, local copies, waits for them, and re-layouts: 11.1 us -> none  [the longest x1 9.69 us: pick_blocks(): flattened[member]]
    concatenate x3 -> x0, other arithmetic: 7.1 us -> none  [the longest x1 5.32 us: on_device(): joined = jnp.concatenate([below_rows, stacked_rows, above_rows], axis=2)]
  transfers between devices with their start and end apart: 6 -> 0, of which waited for: 4 -> 0; matrix products, arithmetic and copies ran while one was open for 12% -> 0% of each run, Pallas kernels for 0% -> 0%
where the time goes in v1:
time: 78.3 us; the launch traced here: 77.3 us
  Pallas kernels  70.3 us (90%)
  local copies, waits for them, and re-layouts  6.36 us (8%)
    pallas_call x1, Pallas kernels, on_device(): pl.pallas_call(functools.partial(kernel, na, nv), out_shape=(jax.ShapeDty...  70.3 us
    unnamed x15, local copies, waits for them, and re-layouts  6.36 us

profile of v1, /device:TPU:1, one launch (start us, length us, event | category | flops | bytes accessed | tf_op | source)
XLA Modules:
  0.0 77.3 jit_solution(5222214404847487521)
XLA Ops:
  0.6 0.0 copy-start.3
  0.6 0.0 copy-start.4
  0.7 0.7 copy.13
  1.4 0.0 copy-start.5
  1.4 0.0 copy-done.3
  1.4 0.0 copy-done.4
  1.4 0.6 copy-done.5
  2.0 0.0 copy-start
  2.0 1.2 %copy-done = f32[4,1,512,128]{3,2,1,0:T(8,128)S(1)} copy-done((f32[4,1,512,128]{3,2,1,0:T(8,128)S(1)}, f32[4,1,512,128]{3,2,1,0:T(8,128)}, u32[]{:S(2)}) %copy-start) | copy-done | bytes 1048600
  3.3 0.0 copy-start.1
  3.3 1.0 %copy-done.1 = f32[2,1,512,128]{3,2,1,0:T(8,128)S(1)} copy-done((f32[2,1,512,128]{3,2,1,0:T(8,128)S(1)}, f32[2,1,512,128]{3,2,1,0:T(8,128)}, u32[]{:S(2)}) %copy-start.1) | copy-done | bytes 524312
  4.3 0.0 copy-start.2
  4.3 0.9 %copy-done.2 = s32[1,512,128]{2,1,0:T(8,128)S(1)} copy-done((s32[1,512,128]{2,1,0:T(8,128)S(1)}, s32[1,512,128]{2,1,0:T(8,128)}, u32[]{:S(2)}) %copy-start.2) | copy-done | bytes 262168
  5.2 70.3 %shard_map.86 = (f32[2,512,128]{2,1,0:T(8,128)S(1)}, f32[4,512,128]{2,1,0:T(8,128)S(1)}) custom-call(f32[2,512,128]{2,1,0:T(8,128)S(1)} %bitcast.15, f32[4,512,128]{2,1,0:T(8,128)S(1)} %bitcast.12, s32[1,512]{1,0:T(1,128)S(1)} %copy-done.3, s32[1,512]{1,0:T(1,128)S(1)} %copy-done.4, s32[6,512]{1,0:T(8,128)S(1)} %bitcast.17, s32[512,128]{1,0:T(8,128)S(1)} %bitcast.16, ...), custom_call_target="tpu_custom_call" | custom-call | tf_op jit(solution)/shard_map/pallas_call | solution.py:336
  75.6 0.8 %copy.16 = f32[2,1,512,128]{3,2,1,0:T(8,128)} copy(f32[2,1,512,128]{3,2,1,0:T(8,128)S(1)} %bitcast.14) | data formatting | bytes 1048576
  76.4 1.0 %copy.17 = f32[4,1,512,128]{3,2,1,0:T(8,128)} copy(f32[4,1,512,128]{3,2,1,0:T(8,128)S(1)} %bitcast.13) | data formatting | bytes 2097152
Async XLA Ops:
  0.6 0.7 copy-start.3
  0.6 0.7 copy-start.4
  1.4 0.7 copy-start.5
  2.0 1.2 %copy-start = (f32[4,1,512,128]{3,2,1,0:T(8,128)S(1)}, f32[4,1,512,128]{3,2,1,0:T(8,128)}, u32[]{:S(2)}) copy-start(f32[4,1,512,128]{3,2,1,0:T(8,128)} %param.8) | copy-start | bytes 3145732
  3.3 1.0 %copy-start.1 = (f32[2,1,512,128]{3,2,1,0:T(8,128)S(1)}, f32[2,1,512,128]{3,2,1,0:T(8,128)}, u32[]{:S(2)}) copy-start(f32[2,1,512,128]{3,2,1,0:T(8,128)} %param.7) | copy-start | bytes 1572868
  4.3 0.9 %copy-start.2 = (s32[1,512,128]{2,1,0:T(8,128)S(1)}, s32[1,512,128]{2,1,0:T(8,128)}, u32[]{:S(2)}) copy-start(s32[1,512,128]{2,1,0:T(8,128)} %param.12) | copy-start | bytes 786436

commit v2 on v1

--- a/solution.py
+++ b/solution.py
@@ -43,8 +43,69 @@
     return hi, (x - hi.astype(F32)).astype(BF16)
 
 
+PIECES = 4
+COUNT_LANE = 45
+
+
+def quarter_shift(yh, zh, edge):
+    return 1 + yh + 2 * zh - edge + 8 * (1 - 2 * yh) + 32 * (1 - 2 * zh)
+
+
+def pack_union(liquid, hydrate, speeds, count):
+    x, z, y = coordinates(liquid.shape[0])
+    core = (y >= 1) & (y <= 2) & (z >= 1) & (z <= 2)
+    kept = []
+    for value, edge in ((liquid, 0), (hydrate, 7)):
+        for yh in range(2):
+            for zh in range(2):
+                value = jnp.where(core & (x == 1 + yh + 2 * zh), roll_lanes(speeds[0], quarter_shift(yh, zh, edge)), value)
+        kept.append(value)
+    lane = lax.broadcasted_iota(jnp.int32, liquid.shape, 1)
+    kept[0] = jnp.where(lane == COUNT_LANE, count, kept[0])
+    third = speeds[1]
+    middle = (z >= 1) & (z <= 2)
+    for zh in range(2):
+        for far in range(2):
+            third = jnp.where(middle & (y == 2 * zh + far),
+                              roll_lanes(speeds[2], 32 * (1 - 2 * zh) + 8 * (2 * zh - 2 * far)), third)
+    return kept[0], kept[1], third
+
+
+def union_tables(first, second, third):
+    rows = first.shape[0]
+    coordinate = coordinates(rows)
+    x, z, y = coordinate
+    lane = lax.broadcasted_iota(jnp.int32, (rows, CELLS), 1)
+    live = (lane.astype(F32) < first[:, COUNT_LANE:COUNT_LANE + 1]).astype(F32)
+    tables = [jnp.zeros((rows, CELLS), F32) for _ in range(5)]
+    for d in range(6):
+        t, k = table_of[d], d // 2
+        edge = axis_extent[k] - 1 if d % 2 == 0 else 0
+        made = tables[t]
+        for member, value in enumerate((first, second, None, live)):
+            p = place_of(d, member)
+            there = coordinate[k] == p
+            if member != 2:
+                made = jnp.where(there, roll_lanes(value, (p - edge) * axis_stride[k]), made)
+            elif k == 0:
+                held = second if edge else first
+                for yh in range(2):
+                    for zh in range(2):
+                        made = jnp.where(there & ((y >> 1) == yh) & ((z >> 1) == zh),
+                                         roll_lanes(held, p - edge - quarter_shift(yh, zh, edge)), made)
+            elif k == 1:
+                made = jnp.where(there, roll_lanes(third, (p - edge) * 32), made)
+            else:
+                far = 1 if edge else 0
+                for zh in range(2):
+                    made = jnp.where(there & ((z >> 1) == zh),
+                                     roll_lanes(third, 8 * (p - 2 * zh - far) - 32 * (1 - 2 * zh)), made)
+        tables[t] = made
+    return tables
+
+
 def kernel(na, nv, frac, mot, home, cnt, nb, phase, rates, fout, mout,
-           cells, mv_send, mv_recv, mv_pay, tab, ax_send, ax_recv, vt_recv, win, acc, rowbuf, cols,
+           cells, mv_send, mv_recv, mv_pay, tab, vt_send, ax_send, ax_recv, vt_recv, win, acc, rowbuf, cols,
            mv_ss, mv_rs, ax_ss, ax_rs, vt_ss, vt_rs):
     slots = frac.shape[1]
     shift = slots.bit_length() - 1
@@ -77,10 +138,12 @@
             src_ref=ax_send.at[s], dst_ref=ax_recv.at[s * 3 + v], send_sem=ax_ss.at[s * 3 + v],
             recv_sem=ax_rs.at[s * 3 + v], device_id=peer, device_id_type=MESH)
 
-    def vertical(s, t, peer):
+    piece = slots // PIECES
+
+    def vertical(s, q, peer):
         return pltpu.make_async_remote_copy(
-            src_ref=tab.at[t], dst_ref=vt_recv.at[s * 5 + t], send_sem=vt_ss.at[s * 5 + t],
-            recv_sem=vt_rs.at[s * 5 + t], device_id=peer, device_id_type=MESH)
+            src_ref=vt_send.at[q], dst_ref=vt_recv.at[s * PIECES + q], send_sem=vt_ss.at[s * PIECES + q],
+            recv_sem=vt_rs.at[s * PIECES + q], device_id=peer, device_id_type=MESH)
 
     slot_row = lax.broadcasted_iota(jnp.int32, (1, slots), 1)
     target = home[...]
@@ -129,8 +192,8 @@
 
         @pl.when(jnp.logical_not(inside(ax, vt - steps[s])))
         def _():
-            for t in range(5):
-                vt_recv[s * 5 + t] = jnp.zeros((slots, CELLS), F32)
+            for q in range(PIECES):
+                vt_recv[s * PIECES + q] = jnp.zeros((3, piece, CELLS), F32)
 
         for v in range(3):
             @pl.when(jnp.logical_not(inside(ax - steps[s], vt - (v - 1))))
@@ -158,9 +221,9 @@
 
     chunk = 64
 
-    @pl.loop(0, slots // chunk)
-    def _(c):
-        start = pl.multiple_of(c * chunk, chunk)
+    def settle(q, c):
+        start = pl.multiple_of(q * piece + c * chunk, chunk)
+        part = pl.ds(pl.multiple_of(c * chunk, chunk), chunk)
         rows = pl.ds(start, chunk)
         at = (lax.broadcasted_iota(jnp.int32, (chunk, CELLS), 0) + start).astype(F32)
         select = (at == arrivals).astype(F32)
@@ -191,12 +254,16 @@
             hi, lo = halves(made)
             win[t, rows, :CELLS] = hi
             win[t, rows, CELLS:] = lo
-
-    for t in range(5):
+        union = pack_union(now[0], now[1], now[2:5], cols[rows, 6:7])
+        for r in range(3):
+            vt_send[q, r, part] = union[r]
+
+    for q in range(PIECES):
+        pl.loop(0, piece // chunk)(functools.partial(settle, q))
         for s in range(2):
             @pl.when(inside(ax, vt + steps[s]))
             def _():
-                vertical(s, t, (ax, vt + steps[s])).start()
+                vertical(s, q, (ax, vt + steps[s])).start()
 
     pick = jnp.concatenate([one_hot(2, MOVES), one_hot(3, MOVES)], axis=0).astype(BF16)
     for t in range(5):
@@ -212,22 +279,18 @@
             def _():
                 axial(s, v, (ax + steps[s], vt + v - 1)).start()
 
-    tall = 128
-
     def gather(t, keys, fresh):
-        @pl.loop(0, slots // tall)
-        def _(c):
-            rows = pl.ds(pl.multiple_of(c * tall, tall), tall)
-            for d in range(6):
-                if table_of[d] != t:
-                    continue
-                match = (cols[rows, d:d + 1] == keys).astype(F32).astype(BF16)
-                both = jnp.dot(match, win[t, :slots], preferred_element_type=F32)
-                both = both[:, :CELLS] + both[:, CELLS:]
-                if fresh:
-                    acc[d, rows] = both
-                else:
-                    acc[d, rows] += both
+        depth = keys.shape[1]
+        for d in range(6):
+            if table_of[d] != t:
+                continue
+            match = (cols[:, d:d + 1] == keys).astype(F32).astype(BF16)
+            both = jnp.dot(match, win[t, :depth], preferred_element_type=F32)
+            both = both[:, :CELLS] + both[:, CELLS:]
+            if fresh:
+                acc[d] = both
+            else:
+                acc[d] += both
 
     for t in range(5):
         gather(t, global_row - 1.0, True)
@@ -263,20 +326,29 @@
         win[t, 6 * PACK:] = jnp.zeros((slots - 6 * PACK, 2 * CELLS), BF16)
         gather(t, ax_keys, False)
 
-    for t in range(5):
+    piece_row = lax.broadcasted_iota(jnp.int32, (1, piece), 1)
+    unpack = 32
+    for q in range(PIECES):
+        keys = []
         for s in range(2):
             @pl.when(inside(ax, vt - steps[s]))
             def _():
-                vertical(s, t, (ax, vt - steps[s])).wait_recv()
-
-            @pl.loop(0, slots // tall)
+                vertical(s, q, (ax, vt - steps[s])).wait_recv()
+
+            @pl.loop(0, piece // unpack)
             def _(c):
-                rows = pl.ds(pl.multiple_of(c * tall, tall), tall)
-                hi, lo = halves(vt_recv[s * 5 + t, rows])
-                win[t, rows, :CELLS] = hi
-                win[t, rows, CELLS:] = lo
-
-            gather(t, (slot_row + ((vt - steps[s]) * total + ax * slots)).astype(F32), False)
+                rows = pl.ds(pl.multiple_of(c * unpack, unpack), unpack)
+                to = pl.ds(pl.multiple_of(s * piece + c * unpack, unpack), unpack)
+                tables = union_tables(*[vt_recv[s * PIECES + q, r, rows] for r in range(3)])
+                for t in range(5):
+                    hi, lo = halves(tables[t])
+                    win[t, to, :CELLS] = hi
+                    win[t, to, CELLS:] = lo
+
+            keys.append((piece_row + ((vt - steps[s]) * total + ax * slots + q * piece)).astype(F32))
+        keys = jnp.concatenate(keys, axis=1)
+        for t in range(5):
+            gather(t, keys, False)
 
     small = 32
 
@@ -323,10 +395,10 @@
             def _():
                 axial(s, v, (ax + steps[s], vt + v - 1)).wait_send()
 
-        for t in range(5):
+        for q in range(PIECES):
             @pl.when(inside(ax, vt + steps[s]))
             def _():
-                vertical(s, t, (ax, vt + steps[s])).wait_send()
+                vertical(s, q, (ax, vt + steps[s])).wait_send()
 
 
 def on_device(fractions, motion_fields, new_home, counts, neighbours, phase_ids, growth_rates):
@@ -344,9 +416,10 @@
             pltpu.VMEM((2, ROWS_MV, CELLS), F32),
             pltpu.VMEM((6, CELLS, CELLS), F32),
             pltpu.VMEM((5, slots, CELLS), F32),
+            pltpu.VMEM((PIECES, 3, slots // PIECES, CELLS), F32),
             pltpu.VMEM((2, ROWS_AX, CELLS), F32),
             pltpu.VMEM((6, ROWS_AX, CELLS), F32),
-            pltpu.VMEM((10, slots, CELLS), F32),
+            pltpu.VMEM((2 * PIECES, 3, slots // PIECES, CELLS), F32),
             pltpu.VMEM((5, slots, 2 * CELLS), BF16),
             pltpu.VMEM((6, slots, CELLS), F32),
             pltpu.VMEM((8, slots), F32),
@@ -355,8 +428,8 @@
             pltpu.SemaphoreType.DMA((2,)),
             pltpu.SemaphoreType.DMA((6,)),
             pltpu.SemaphoreType.DMA((6,)),
-            pltpu.SemaphoreType.DMA((10,)),
-            pltpu.SemaphoreType.DMA((10,)),
+            pltpu.SemaphoreType.DMA((2 * PIECES,)),
+            pltpu.SemaphoreType.DMA((2 * PIECES,)),
         ],
         compiler_params=pltpu.CompilerParams(
             collective_id=0, has_side_effects=True, vmem_limit_bytes=40 * 1024 * 1024),

time: 78.3 us -> 58.6 us (0.75)
  Pallas kernels: 70.3 us -> 50.6 us
    pallas_call x1, Pallas kernels: 70.3 us -> 50.6 us  [on_device(): pl.pallas_call(functools.partial(kernel, na, nv), out_shape=(jax.ShapeDty...]
where the time goes in v2:
time: 58.6 us; the launch traced here: 57.6 us
  Pallas kernels  50.6 us (86%)
  local copies, waits for them, and re-layouts  6.36 us (11%)
  between operations  0.66 us (1%)
    pallas_call x1, Pallas kernels, on_device(): pl.pallas_call(functools.partial(kernel, na, nv), out_shape=(jax.ShapeDty...  50.6 us
    unnamed x15, local copies, waits for them, and re-layouts  6.36 us

profile of v2, /device:TPU:1, one launch (start us, length us, event | category | flops | bytes accessed | tf_op | source)
XLA Modules:
  0.0 57.6 jit_solution(15225525885537183870)
XLA Ops:
  0.6 0.0 copy-start.3
  0.6 0.0 copy-start.4
  0.7 0.7 %copy.13 = s32[6,1,512]{2,0,1:T(8,128)S(1)} copy(s32[6,1,512]{2,1,0:T(1,128)} %param.11) | data formatting | bytes 24576
  1.4 0.0 copy-start.5
  1.4 0.0 copy-done.3
  1.4 0.0 copy-done.4
  1.4 0.6 %copy-done.5 = f32[4]{0:T(128)S(1)} copy-done((f32[4]{0:T(128)S(1)}, f32[4]{0:T(128)}, u32[]{:S(2)}) %copy-start.5) | copy-done | bytes 40
  2.0 0.0 copy-start
  2.0 1.2 %copy-done = f32[4,1,512,128]{3,2,1,0:T(8,128)S(1)} copy-done((f32[4,1,512,128]{3,2,1,0:T(8,128)S(1)}, f32[4,1,512,128]{3,2,1,0:T(8,128)}, u32[]{:S(2)}) %copy-start) | copy-done | bytes 1048600
  3.3 0.0 copy-start.1
  3.3 1.0 %copy-done.1 = f32[2,1,512,128]{3,2,1,0:T(8,128)S(1)} copy-done((f32[2,1,512,128]{3,2,1,0:T(8,128)S(1)}, f32[2,1,512,128]{3,2,1,0:T(8,128)}, u32[]{:S(2)}) %copy-start.1) | copy-done | bytes 524312
  4.3 0.0 copy-start.2
  4.3 0.9 %copy-done.2 = s32[1,512,128]{2,1,0:T(8,128)S(1)} copy-done((s32[1,512,128]{2,1,0:T(8,128)S(1)}, s32[1,512,128]{2,1,0:T(8,128)}, u32[]{:S(2)}) %copy-start.2) | copy-done | bytes 262168
  5.2 50.6 %shard_map.86 = (f32[2,512,128]{2,1,0:T(8,128)S(1)}, f32[4,512,128]{2,1,0:T(8,128)S(1)}) custom-call(f32[2,512,128]{2,1,0:T(8,128)S(1)} %bitcast.15, f32[4,512,128]{2,1,0:T(8,128)S(1)} %bitcast.12, s32[1,512]{1,0:T(1,128)S(1)} %copy-done.3, s32[1,512]{1,0:T(1,128)S(1)} %copy-done.4, s32[6,512]{1,0:T(8,128)S(1)} %bitcast.17, s32[512,128]{1,0:T(8,128)S(1)} %bitcast.16, ...), custom_call_target="tpu_custom_call" | custom-call | tf_op jit(solution)/shard_map/pallas_call | solution.py:408
  55.9 0.8 %copy.16 = f32[2,1,512,128]{3,2,1,0:T(8,128)} copy(f32[2,1,512,128]{3,2,1,0:T(8,128)S(1)} %bitcast.14) | data formatting | bytes 1048576
  56.6 1.0 %copy.17 = f32[4,1,512,128]{3,2,1,0:T(8,128)} copy(f32[4,1,512,128]{3,2,1,0:T(8,128)S(1)} %bitcast.13) | data formatting | bytes 2097152
Async XLA Ops:
  0.6 0.7 %copy-start.3 = (s32[1,512]{1,0:T(1,128)S(1)}, s32[1,512]{1,0:T(1,128)}, u32[]{:S(2)}) copy-start(s32[1,512]{1,0:T(1,128)} %home.1) | copy-start | bytes 6148
  0.6 0.7 %copy-start.4 = (s32[1,512]{1,0:T(1,128)S(1)}, s32[1,512]{1,0:T(1,128)}, u32[]{:S(2)}) copy-start(s32[1,512]{1,0:T(1,128)} %cnt.1) | copy-start | bytes 6148
  1.4 0.7 %copy-start.5 = (f32[4]{0:T(128)S(1)}, f32[4]{0:T(128)}, u32[]{:S(2)}) copy-start(f32[4]{0:T(128)} %rates.1) | copy-start | bytes 52
  2.0 1.2 %copy-start = (f32[4,1,512,128]{3,2,1,0:T(8,128)S(1)}, f32[4,1,512,128]{3,2,1,0:T(8,128)}, u32[]{:S(2)}) copy-start(f32[4,1,512,128]{3,2,1,0:T(8,128)} %param.8) | copy-start | bytes 3145732
  3.3 1.0 %copy-start.1 = (f32[2,1,512,128]{3,2,1,0:T(8,128)S(1)}, f32[2,1,512,128]{3,2,1,0:T(8,128)}, u32[]{:S(2)}) copy-start(f32[2,1,512,128]{3,2,1,0:T(8,128)} %param.7) | copy-start | bytes 1572868
  4.3 0.9 %copy-start.2 = (s32[1,512,128]{2,1,0:T(8,128)S(1)}, s32[1,512,128]{2,1,0:T(8,128)}, u32[]{:S(2)}) copy-start(s32[1,512,128]{2,1,0:T(8,128)} %param.12) | copy-start | bytes 786436

commit v3 on v2

--- a/solution.py
+++ b/solution.py
@@ -20,7 +20,7 @@
 time_step = 0.25
 table_of = (0, 0, 1, 2, 3, 4)
 PACK = SPAN + MOVES
-ROWS_AX = 5 * PACK + 8
+ROWS_AX = 3 * PACK + 8
 ROWS_MV = 6 * MOVES + 8
 
 
@@ -105,7 +105,7 @@
 
 
 def kernel(na, nv, frac, mot, home, cnt, nb, phase, rates, fout, mout,
-           cells, mv_send, mv_recv, mv_pay, tab, vt_send, ax_send, ax_recv, vt_recv, win, acc, rowbuf, cols,
+           cells, mv_send, mv_recv, mv_pay, vt_send, ax_send, ax_recv, vt_recv, win, acc, rowbuf, cols,
            mv_ss, mv_rs, ax_ss, ax_rs, vt_ss, vt_rs):
     slots = frac.shape[1]
     shift = slots.bit_length() - 1
@@ -160,10 +160,6 @@
     rank = jnp.dot(mask8.astype(BF16), before.astype(F32).astype(BF16), preferred_element_type=F32)
     rank = jnp.where(mask8 > 0.0, rank, -1.0)
 
-    rowbuf[...] = jnp.concatenate(
-        [linked.astype(F32), cnt[...].astype(F32), jnp.zeros((1, slots), F32)], axis=0)
-    cols[...] = rowbuf[...].T
-
     def one_hot(which, rows):
         m = (lax.broadcasted_iota(jnp.int32, (rows, slots), 0) & (MOVES - 1)).astype(F32)
         return (rank[which:which + 1] == m).astype(F32)
@@ -183,7 +179,19 @@
             mv_send[s, f * MOVES:(f + 1) * MOVES] = packed[s * MOVES:(s + 1) * MOVES]
     for s in range(2):
         mv_send[s, 6 * MOVES:] = names(s, target_slot)
-        ax_send[s, 5 * PACK:] = names(2 + s, global_row)
+
+    pl.semaphore_wait(barrier, greeted)
+    for s in range(2):
+        @pl.when(inside(ax + steps[s], vt))
+        def _():
+            mover(s, (ax + steps[s], vt)).start()
+
+    rowbuf[...] = jnp.concatenate(
+        [linked.astype(F32), cnt[...].astype(F32), jnp.zeros((1, slots), F32)], axis=0)
+    cols[...] = rowbuf[...].T
+
+    for s in range(2):
+        ax_send[s, 3 * PACK:] = names(2 + s, global_row)
 
     for s in range(2):
         @pl.when(jnp.logical_not(inside(ax - steps[s], vt)))
@@ -199,12 +207,6 @@
             @pl.when(jnp.logical_not(inside(ax - steps[s], vt - (v - 1))))
             def _():
                 ax_recv[s * 3 + v] = jnp.zeros((ROWS_AX, CELLS), F32)
-
-    pl.semaphore_wait(barrier, greeted)
-    for s in range(2):
-        @pl.when(inside(ax + steps[s], vt))
-        def _():
-            mover(s, (ax + steps[s], vt)).start()
 
     mv_pay[...] = jnp.zeros_like(mv_pay)
     for s in range(2):
@@ -250,7 +252,6 @@
                 for member, value in enumerate((now[0], now[1], now[2 + k], live)):
                     p = place_of(d, member)
                     made = jnp.where(coordinate[k] == p, roll_lanes(value, (p - edge) * axis_stride[k]), made)
-            tab[t, rows] = made
             hi, lo = halves(made)
             win[t, rows, :CELLS] = hi
             win[t, rows, CELLS:] = lo
@@ -265,14 +266,15 @@
             def _():
                 vertical(s, q, (ax, vt + steps[s])).start()
 
-    pick = jnp.concatenate([one_hot(2, MOVES), one_hot(3, MOVES)], axis=0).astype(BF16)
-    for t in range(5):
-        both = jnp.dot(pick, win[t, :slots], preferred_element_type=F32)
-        packed = both[:, :CELLS] + both[:, CELLS:]
+    pick = jnp.concatenate([one_hot(2, MOVES), one_hot(3, MOVES)], axis=0)
+    for r in range(3):
+        packed = jnp.zeros((2 * MOVES, CELLS), F32)
+        for q in range(PIECES):
+            packed = packed + jnp.dot(pick[:, q * piece:(q + 1) * piece], vt_send[q, r], precision=HIGH,
+                                      preferred_element_type=F32)
         for s in range(2):
-            first = slots - SPAN if s == 0 else 0
-            ax_send[s, t * PACK:t * PACK + SPAN] = tab[t, first:first + SPAN]
-            ax_send[s, t * PACK + SPAN:(t + 1) * PACK] = packed[s * MOVES:(s + 1) * MOVES]
+            ax_send[s, r * PACK:r * PACK + SPAN] = vt_send[PIECES - 1, r, piece - SPAN:] if s == 0 else vt_send[0, r, :SPAN]
+            ax_send[s, r * PACK + SPAN:(r + 1) * PACK] = packed[s * MOVES:(s + 1) * MOVES]
     for s in range(2):
         for v in range(3):
             @pl.when(inside(ax + steps[s], vt + v - 1))
@@ -310,19 +312,24 @@
             layer_keys = jnp.where(which == w, (within + base).astype(F32), layer_keys)
     other_keys = jnp.full((1, CELLS), -2.0, F32)
     for w in range(6):
-        row = ax_recv[w, 5 * PACK:5 * PACK + 1]
+        row = ax_recv[w, 3 * PACK:3 * PACK + 1]
         row = jnp.where(row > 0.0, row - 1.0, -2.0)
         other_keys = jnp.where((lane1 >> 4) == w, row, other_keys)
     ax_keys = jnp.concatenate([layer_keys[:, :6 * SPAN], other_keys], axis=1)
+
+    @pl.loop(0, 6)
+    def _(w):
+        tables = union_tables(*[ax_recv[w, r * PACK:(r + 1) * PACK] for r in range(3)])
+        layer = pl.ds(pl.multiple_of(w * SPAN, SPAN), SPAN)
+        rest = pl.ds(pl.multiple_of(6 * SPAN + w * MOVES, MOVES), MOVES)
+        for t in range(5):
+            hi, lo = halves(tables[t])
+            win[t, layer, :CELLS] = hi[:SPAN]
+            win[t, layer, CELLS:] = lo[:SPAN]
+            win[t, rest, :CELLS] = hi[SPAN:]
+            win[t, rest, CELLS:] = lo[SPAN:]
+
     for t in range(5):
-        for w in range(6):
-            hi, lo = halves(ax_recv[w, t * PACK:t * PACK + SPAN])
-            win[t, w * SPAN:(w + 1) * SPAN, :CELLS] = hi
-            win[t, w * SPAN:(w + 1) * SPAN, CELLS:] = lo
-            first = 6 * SPAN + w * MOVES
-            hi, lo = halves(ax_recv[w, t * PACK + SPAN:(t + 1) * PACK])
-            win[t, first:first + MOVES, :CELLS] = hi
-            win[t, first:first + MOVES, CELLS:] = lo
         win[t, 6 * PACK:] = jnp.zeros((slots - 6 * PACK, 2 * CELLS), BF16)
         gather(t, ax_keys, False)
 
@@ -415,7 +422,6 @@
             pltpu.VMEM((2, ROWS_MV, CELLS), F32),
             pltpu.VMEM((2, ROWS_MV, CELLS), F32),
             pltpu.VMEM((6, CELLS, CELLS), F32),
-            pltpu.VMEM((5, slots, CELLS), F32),
             pltpu.VMEM((PIECES, 3, slots // PIECES, CELLS), F32),
             pltpu.VMEM((2, ROWS_AX, CELLS), F32),
             pltpu.VMEM((6, ROWS_AX, CELLS), F32),

time: 58.6 us -> 57.1 us (0.974)
  Pallas kernels: 50.6 us -> 49.7 us
    pallas_call x1, Pallas kernels: 50.6 us -> 49.7 us  [on_device(): pl.pallas_call(functools.partial(kernel, na, nv), out_shape=(jax.ShapeDty...]
where the time goes in v3:
time: 57.1 us; the launch traced here: 56.7 us
  Pallas kernels  49.7 us (87%)
  local copies, waits for them, and re-layouts  6.36 us (11%)
  between operations  0.66 us (1%)
    pallas_call x1, Pallas kernels, on_device(): pl.pallas_call(functools.partial(kernel, na, nv), out_shape=(jax.ShapeDty...  49.7 us
    unnamed x15, local copies, waits for them, and re-layouts  6.36 us

profile of v3, /device:TPU:1, one launch (start us, length us, event | category | flops | bytes accessed | tf_op | source)
XLA Modules:
  0.0 56.7 jit_solution(18046060630244215473)
XLA Ops:
  0.6 0.0 copy-start.3
  0.6 0.0 copy-start.4
  0.7 0.7 %copy.13 = s32[6,1,512]{2,0,1:T(8,128)S(1)} copy(s32[6,1,512]{2,1,0:T(1,128)} %param.11) | data formatting | bytes 24576
  1.4 0.0 copy-start.5
  1.4 0.0 copy-done.3
  1.4 0.0 copy-done.4
  1.4 0.6 %copy-done.5 = f32[4]{0:T(128)S(1)} copy-done((f32[4]{0:T(128)S(1)}, f32[4]{0:T(128)}, u32[]{:S(2)}) %copy-start.5) | copy-done | bytes 40
  2.0 0.0 copy-start
  2.0 1.2 %copy-done = f32[4,1,512,128]{3,2,1,0:T(8,128)S(1)} copy-done((f32[4,1,512,128]{3,2,1,0:T(8,128)S(1)}, f32[4,1,512,128]{3,2,1,0:T(8,128)}, u32[]{:S(2)}) %copy-start) | copy-done | bytes 1048600
  3.3 0.0 copy-start.1
  3.3 1.0 %copy-done.1 = f32[2,1,512,128]{3,2,1,0:T(8,128)S(1)} copy-done((f32[2,1,512,128]{3,2,1,0:T(8,128)S(1)}, f32[2,1,512,128]{3,2,1,0:T(8,128)}, u32[]{:S(2)}) %copy-start.1) | copy-done | bytes 524312
  4.3 0.0 copy-start.2
  4.3 0.9 %copy-done.2 = s32[1,512,128]{2,1,0:T(8,128)S(1)} copy-done((s32[1,512,128]{2,1,0:T(8,128)S(1)}, s32[1,512,128]{2,1,0:T(8,128)}, u32[]{:S(2)}) %copy-start.2) | copy-done | bytes 262168
  5.2 49.7 %shard_map.86 = (f32[2,512,128]{2,1,0:T(8,128)S(1)}, f32[4,512,128]{2,1,0:T(8,128)S(1)}) custom-call(f32[2,512,128]{2,1,0:T(8,128)S(1)} %bitcast.15, f32[4,512,128]{2,1,0:T(8,128)S(1)} %bitcast.12, s32[1,512]{1,0:T(1,128)S(1)} %copy-done.3, s32[1,512]{1,0:T(1,128)S(1)} %copy-done.4, s32[6,512]{1,0:T(8,128)S(1)} %bitcast.17, s32[512,128]{1,0:T(8,128)S(1)} %bitcast.16, ...), custom_call_target="tpu_custom_call" | custom-call | tf_op jit(solution)/shard_map/pallas_call | solution.py:415
  54.9 0.8 %copy.16 = f32[2,1,512,128]{3,2,1,0:T(8,128)} copy(f32[2,1,512,128]{3,2,1,0:T(8,128)S(1)} %bitcast.14) | data formatting | bytes 1048576
  55.7 1.0 %copy.17 = f32[4,1,512,128]{3,2,1,0:T(8,128)} copy(f32[4,1,512,128]{3,2,1,0:T(8,128)S(1)} %bitcast.13) | data formatting | bytes 2097152
Async XLA Ops:
  0.6 0.7 %copy-start.3 = (s32[1,512]{1,0:T(1,128)S(1)}, s32[1,512]{1,0:T(1,128)}, u32[]{:S(2)}) copy-start(s32[1,512]{1,0:T(1,128)} %home.1) | copy-start | bytes 6148
  0.6 0.7 %copy-start.4 = (s32[1,512]{1,0:T(1,128)S(1)}, s32[1,512]{1,0:T(1,128)}, u32[]{:S(2)}) copy-start(s32[1,512]{1,0:T(1,128)} %cnt.1) | copy-start | bytes 6148
  1.4 0.7 %copy-start.5 = (f32[4]{0:T(128)S(1)}, f32[4]{0:T(128)}, u32[]{:S(2)}) copy-start(f32[4]{0:T(128)} %rates.1) | copy-start | bytes 52
  2.0 1.2 %copy-start = (f32[4,1,512,128]{3,2,1,0:T(8,128)S(1)}, f32[4,1,512,128]{3,2,1,0:T(8,128)}, u32[]{:S(2)}) copy-start(f32[4,1,512,128]{3,2,1,0:T(8,128)} %param.8) | copy-start | bytes 3145732
  3.3 1.0 %copy-start.1 = (f32[2,1,512,128]{3,2,1,0:T(8,128)S(1)}, f32[2,1,512,128]{3,2,1,0:T(8,128)}, u32[]{:S(2)}) copy-start(f32[2,1,512,128]{3,2,1,0:T(8,128)} %param.7) | copy-start | bytes 1572868
  4.3 0.9 %copy-start.2 = (s32[1,512,128]{2,1,0:T(8,128)S(1)}, s32[1,512,128]{2,1,0:T(8,128)}, u32[]{:S(2)}) copy-start(s32[1,512,128]{2,1,0:T(8,128)} %param.12) | copy-start | bytes 786436

commit v4 on v3

--- a/solution.py
+++ b/solution.py
@@ -22,6 +22,7 @@
 PACK = SPAN + MOVES
 ROWS_AX = 3 * PACK + 8
 ROWS_MV = 6 * MOVES + 8
+ROWS_FIX = 6 * MOVES + 24
 
 
 def place_of(direction, member):
@@ -105,8 +106,8 @@
 
 
 def kernel(na, nv, frac, mot, home, cnt, nb, phase, rates, fout, mout,
-           cells, mv_send, mv_recv, mv_pay, vt_send, ax_send, ax_recv, vt_recv, win, acc, rowbuf, cols,
-           mv_ss, mv_rs, ax_ss, ax_rs, vt_ss, vt_rs):
+           cells, mv_send, mv_recv, mv_pay, vt_send, settled, fix_send, fix_recv, ax_send, ax_recv, vt_recv, win, acc, rowbuf, cols,
+           fix_ss, fix_rs, mv_ss, mv_rs, ax_ss, ax_rs, vt_ss, vt_rs):
     slots = frac.shape[1]
     shift = slots.bit_length() - 1
     total = slots * na
@@ -144,6 +145,11 @@
         return pltpu.make_async_remote_copy(
             src_ref=vt_send.at[q], dst_ref=vt_recv.at[s * PIECES + q], send_sem=vt_ss.at[s * PIECES + q],
             recv_sem=vt_rs.at[s * PIECES + q], device_id=peer, device_id_type=MESH)
+
+    def fixes(s, peer):
+        return pltpu.make_async_remote_copy(
+            src_ref=fix_send, dst_ref=fix_recv.at[s], send_sem=fix_ss.at[s], recv_sem=fix_rs.at[s],
+            device_id=peer, device_id_type=MESH)
 
     slot_row = lax.broadcasted_iota(jnp.int32, (1, slots), 1)
     target = home[...]
@@ -189,6 +195,21 @@
     rowbuf[...] = jnp.concatenate(
         [linked.astype(F32), cnt[...].astype(F32), jnp.zeros((1, slots), F32)], axis=0)
     cols[...] = rowbuf[...].T
+
+    early = 64
+    for q in range(PIECES):
+        @pl.loop(0, piece // early)
+        def _(c):
+            rows = pl.ds(pl.multiple_of(q * piece + c * early, early), early)
+            part = pl.ds(pl.multiple_of(c * early, early), early)
+            union = pack_union(frac[0, rows], frac[1, rows], [mot[k, rows] for k in range(3)], cols[rows, 6:7])
+            for r in range(3):
+                vt_send[q, r, part] = union[r]
+
+        for s in range(2):
+            @pl.when(inside(ax, vt + steps[s]))
+            def _():
+                vertical(s, q, (ax, vt + steps[s])).start()
 
     for s in range(2):
         ax_send[s, 3 * PACK:] = names(2 + s, global_row)
@@ -257,24 +278,34 @@
             win[t, rows, CELLS:] = lo
         union = pack_union(now[0], now[1], now[2:5], cols[rows, 6:7])
         for r in range(3):
-            vt_send[q, r, part] = union[r]
+            settled[q, r, part] = union[r]
 
     for q in range(PIECES):
         pl.loop(0, piece // chunk)(functools.partial(settle, q))
-        for s in range(2):
-            @pl.when(inside(ax, vt + steps[s]))
-            def _():
-                vertical(s, q, (ax, vt + steps[s])).start()
-
-    pick = jnp.concatenate([one_hot(2, MOVES), one_hot(3, MOVES)], axis=0)
+
+    pick = jnp.concatenate([one_hot(2, MOVES), one_hot(3, MOVES), one_hot(0, MOVES), one_hot(1, MOVES)], axis=0)
     for r in range(3):
-        packed = jnp.zeros((2 * MOVES, CELLS), F32)
+        packed = jnp.zeros((4 * MOVES, CELLS), F32)
         for q in range(PIECES):
-            packed = packed + jnp.dot(pick[:, q * piece:(q + 1) * piece], vt_send[q, r], precision=HIGH,
+            packed = packed + jnp.dot(pick[:, q * piece:(q + 1) * piece], settled[q, r], precision=HIGH,
                                       preferred_element_type=F32)
         for s in range(2):
-            ax_send[s, r * PACK:r * PACK + SPAN] = vt_send[PIECES - 1, r, piece - SPAN:] if s == 0 else vt_send[0, r, :SPAN]
+            ax_send[s, r * PACK:r * PACK + SPAN] = settled[PIECES - 1, r, piece - SPAN:] if s == 0 else settled[0, r, :SPAN]
             ax_send[s, r * PACK + SPAN:(r + 1) * PACK] = packed[s * MOVES:(s + 1) * MOVES]
+        fix_send[r * 2 * MOVES:(r + 1) * 2 * MOVES] = packed[2 * MOVES:]
+    for s in range(2):
+        fix_send[6 * MOVES + 8 * s:6 * MOVES + 8 * s + 8] = names(s, global_row)
+    replaced = masks[0] + masks[1]
+    fix_send[6 * MOVES + 16:] = jnp.concatenate(
+        [replaced[:, q * piece:(q + 1) * piece] for q in range(PIECES)] + [jnp.zeros((8 - PIECES, piece), F32)], axis=0)
+    for s in range(2):
+        @pl.when(inside(ax, vt + steps[s]))
+        def _():
+            fixes(s, (ax, vt + steps[s])).start()
+
+        @pl.when(jnp.logical_not(inside(ax, vt - steps[s])))
+        def _():
+            fix_recv[s] = jnp.zeros((ROWS_FIX, CELLS), F32)
     for s in range(2):
         for v in range(3):
             @pl.when(inside(ax + steps[s], vt + v - 1))
@@ -333,6 +364,25 @@
         win[t, 6 * PACK:] = jnp.zeros((slots - 6 * PACK, 2 * CELLS), BF16)
         gather(t, ax_keys, False)
 
+    fix_keys = jnp.full((1, CELLS), -2.0, F32)
+    for s in range(2):
+        @pl.when(inside(ax, vt - steps[s]))
+        def _():
+            fixes(s, (ax, vt - steps[s])).wait_recv()
+
+        tables = union_tables(*[fix_recv[s, r * 2 * MOVES:(r + 1) * 2 * MOVES] for r in range(3)])
+        for t in range(5):
+            hi, lo = halves(tables[t])
+            win[t, s * 2 * MOVES:(s + 1) * 2 * MOVES, :CELLS] = hi
+            win[t, s * 2 * MOVES:(s + 1) * 2 * MOVES, CELLS:] = lo
+        for way in range(2):
+            row = fix_recv[s, 6 * MOVES + 8 * way:6 * MOVES + 8 * way + 1]
+            row = jnp.where(row > 0.0, row - 1.0, -2.0)
+            fix_keys = jnp.where((lane1 >> 4) == 2 * s + way, row, fix_keys)
+    for t in range(5):
+        win[t, 4 * MOVES:CELLS] = jnp.zeros((CELLS - 4 * MOVES, 2 * CELLS), BF16)
+        gather(t, fix_keys, False)
+
     piece_row = lax.broadcasted_iota(jnp.int32, (1, piece), 1)
     unpack = 32
     for q in range(PIECES):
@@ -352,7 +402,8 @@
                     win[t, to, :CELLS] = hi
                     win[t, to, CELLS:] = lo
 
-            keys.append((piece_row + ((vt - steps[s]) * total + ax * slots + q * piece)).astype(F32))
+            named = (piece_row + ((vt - steps[s]) * total + ax * slots + q * piece)).astype(F32)
+            keys.append(jnp.where(fix_recv[s, 6 * MOVES + 16 + q:6 * MOVES + 17 + q] > 0.0, -2.0, named))
         keys = jnp.concatenate(keys, axis=1)
         for t in range(5):
             gather(t, keys, False)
@@ -402,6 +453,10 @@
             def _():
                 axial(s, v, (ax + steps[s], vt + v - 1)).wait_send()
 
+        @pl.when(inside(ax, vt + steps[s]))
+        def _():
+            fixes(s, (ax, vt + steps[s])).wait_send()
+
         for q in range(PIECES):
             @pl.when(inside(ax, vt + steps[s]))
             def _():
@@ -423,6 +478,9 @@
             pltpu.VMEM((2, ROWS_MV, CELLS), F32),
             pltpu.VMEM((6, CELLS, CELLS), F32),
             pltpu.VMEM((PIECES, 3, slots // PIECES, CELLS), F32),
+            pltpu.VMEM((PIECES, 3, slots // PIECES, CELLS), F32),
+            pltpu.VMEM((ROWS_FIX, CELLS), F32),
+            pltpu.VMEM((2, ROWS_FIX, CELLS), F32),
             pltpu.VMEM((2, ROWS_AX, CELLS), F32),
             pltpu.VMEM((6, ROWS_AX, CELLS), F32),
             pltpu.VMEM((2 * PIECES, 3, slots // PIECES, CELLS), F32),
@@ -430,6 +488,8 @@
             pltpu.VMEM((6, slots, CELLS), F32),
             pltpu.VMEM((8, slots), F32),
             pltpu.VMEM((slots, 8), F32),
+            pltpu.SemaphoreType.DMA((2,)),
+            pltpu.SemaphoreType.DMA((2,)),
             pltpu.SemaphoreType.DMA((2,)),
             pltpu.SemaphoreType.DMA((2,)),
             pltpu.SemaphoreType.DMA((6,)),

time: 57.1 us -> 55.8 us (0.977)
  Pallas kernels: 49.7 us -> 48.4 us
    pallas_call x1, Pallas kernels: 49.7 us -> 48.4 us  [on_device(): pl.pallas_call(functools.partial(kernel, na, nv), out_shape=(jax.ShapeDty...]
where the time goes in v4:
time: 55.8 us; the launch traced here: 55.5 us
  Pallas kernels  48.4 us (87%)
  local copies, waits for them, and re-layouts  6.36 us (11%)
  between operations  0.66 us (1%)
    pallas_call x1, Pallas kernels, on_device(): pl.pallas_call(functools.partial(kernel, na, nv), out_shape=(jax.ShapeDty...  48.4 us
    unnamed x15, local copies, waits for them, and re-layouts  6.36 us

profile of v4, /device:TPU:1, one launch (start us, length us, event | category | flops | bytes accessed | tf_op | source)
XLA Modules:
  0.0 55.5 jit_solution(17541034128191552781)
XLA Ops:
  0.6 0.0 copy-start.3
  0.6 0.0 copy-start.4
  0.7 0.7 %copy.13 = s32[6,1,512]{2,0,1:T(8,128)S(1)} copy(s32[6,1,512]{2,1,0:T(1,128)} %param.11) | data formatting | bytes 24576
  1.4 0.0 copy-start.5
  1.4 0.0 copy-done.3
  1.4 0.0 copy-done.4
  1.4 0.6 %copy-done.5 = f32[4]{0:T(128)S(1)} copy-done((f32[4]{0:T(128)S(1)}, f32[4]{0:T(128)}, u32[]{:S(2)}) %copy-start.5) | copy-done | bytes 40
  2.0 0.0 copy-start
  2.0 1.2 %copy-done = f32[4,1,512,128]{3,2,1,0:T(8,128)S(1)} copy-done((f32[4,1,512,128]{3,2,1,0:T(8,128)S(1)}, f32[4,1,512,128]{3,2,1,0:T(8,128)}, u32[]{:S(2)}) %copy-start) | copy-done | bytes 1048600
  3.3 0.0 copy-start.1
  3.3 1.0 %copy-done.1 = f32[2,1,512,128]{3,2,1,0:T(8,128)S(1)} copy-done((f32[2,1,512,128]{3,2,1,0:T(8,128)S(1)}, f32[2,1,512,128]{3,2,1,0:T(8,128)}, u32[]{:S(2)}) %copy-start.1) | copy-done | bytes 524312
  4.3 0.0 copy-start.2
  4.3 0.9 %copy-done.2 = s32[1,512,128]{2,1,0:T(8,128)S(1)} copy-done((s32[1,512,128]{2,1,0:T(8,128)S(1)}, s32[1,512,128]{2,1,0:T(8,128)}, u32[]{:S(2)}) %copy-start.2) | copy-done | bytes 262168
  5.2 48.4 %shard_map.86 = (f32[2,512,128]{2,1,0:T(8,128)S(1)}, f32[4,512,128]{2,1,0:T(8,128)S(1)}) custom-call(f32[2,512,128]{2,1,0:T(8,128)S(1)} %bitcast.15, f32[4,512,128]{2,1,0:T(8,128)S(1)} %bitcast.12, s32[1,512]{1,0:T(1,128)S(1)} %copy-done.3, s32[1,512]{1,0:T(1,128)S(1)} %copy-done.4, s32[6,512]{1,0:T(8,128)S(1)} %bitcast.17, s32[512,128]{1,0:T(8,128)S(1)} %bitcast.16, ...), custom_call_target="tpu_custom_call" | custom-call | tf_op jit(solution)/shard_map/pallas_call | solution.py:470
  53.7 0.8 %copy.16 = f32[2,1,512,128]{3,2,1,0:T(8,128)} copy(f32[2,1,512,128]{3,2,1,0:T(8,128)S(1)} %bitcast.14) | data formatting | bytes 1048576
  54.5 1.0 %copy.17 = f32[4,1,512,128]{3,2,1,0:T(8,128)} copy(f32[4,1,512,128]{3,2,1,0:T(8,128)S(1)} %bitcast.13) | data formatting | bytes 2097152
Async XLA Ops:
  0.6 0.7 %copy-start.3 = (s32[1,512]{1,0:T(1,128)S(1)}, s32[1,512]{1,0:T(1,128)}, u32[]{:S(2)}) copy-start(s32[1,512]{1,0:T(1,128)} %home.1) | copy-start | bytes 6148
  0.6 0.7 %copy-start.4 = (s32[1,512]{1,0:T(1,128)S(1)}, s32[1,512]{1,0:T(1,128)}, u32[]{:S(2)}) copy-start(s32[1,512]{1,0:T(1,128)} %cnt.1) | copy-start | bytes 6148
  1.4 0.7 %copy-start.5 = (f32[4]{0:T(128)S(1)}, f32[4]{0:T(128)}, u32[]{:S(2)}) copy-start(f32[4]{0:T(128)} %rates.1) | copy-start | bytes 52
  2.0 1.2 %copy-start = (f32[4,1,512,128]{3,2,1,0:T(8,128)S(1)}, f32[4,1,512,128]{3,2,1,0:T(8,128)}, u32[]{:S(2)}) copy-start(f32[4,1,512,128]{3,2,1,0:T(8,128)} %param.8) | copy-start | bytes 3145732
  3.3 1.0 %copy-start.1 = (f32[2,1,512,128]{3,2,1,0:T(8,128)S(1)}, f32[2,1,512,128]{3,2,1,0:T(8,128)}, u32[]{:S(2)}) copy-start(f32[2,1,512,128]{3,2,1,0:T(8,128)} %param.7) | copy-start | bytes 1572868
  4.3 0.9 %copy-start.2 = (s32[1,512,128]{2,1,0:T(8,128)S(1)}, s32[1,512,128]{2,1,0:T(8,128)}, u32[]{:S(2)}) copy-start(s32[1,512,128]{2,1,0:T(8,128)} %param.12) | copy-start | bytes 786436

commit v5 on v4

--- a/solution.py
+++ b/solution.py
@@ -328,42 +328,6 @@
     for t in range(5):
         gather(t, global_row - 1.0, True)
 
-    for s in range(2):
-        for v in range(3):
-            @pl.when(inside(ax - steps[s], vt - (v - 1)))
-            def _():
-                axial(s, v, (ax - steps[s], vt - (v - 1))).wait_recv()
-    layer_keys = jnp.full((1, slots), -2.0, F32)
-    which = slot_row >> (SPAN.bit_length() - 1)
-    within = slot_row & (SPAN - 1)
-    for s in range(2):
-        for v in range(3):
-            w = s * 3 + v
-            base = (vt - (v - 1)) * total + (ax - steps[s]) * slots + (slots - SPAN if s == 0 else 0)
-            layer_keys = jnp.where(which == w, (within + base).astype(F32), layer_keys)
-    other_keys = jnp.full((1, CELLS), -2.0, F32)
-    for w in range(6):
-        row = ax_recv[w, 3 * PACK:3 * PACK + 1]
-        row = jnp.where(row > 0.0, row - 1.0, -2.0)
-        other_keys = jnp.where((lane1 >> 4) == w, row, other_keys)
-    ax_keys = jnp.concatenate([layer_keys[:, :6 * SPAN], other_keys], axis=1)
-
-    @pl.loop(0, 6)
-    def _(w):
-        tables = union_tables(*[ax_recv[w, r * PACK:(r + 1) * PACK] for r in range(3)])
-        layer = pl.ds(pl.multiple_of(w * SPAN, SPAN), SPAN)
-        rest = pl.ds(pl.multiple_of(6 * SPAN + w * MOVES, MOVES), MOVES)
-        for t in range(5):
-            hi, lo = halves(tables[t])
-            win[t, layer, :CELLS] = hi[:SPAN]
-            win[t, layer, CELLS:] = lo[:SPAN]
-            win[t, rest, :CELLS] = hi[SPAN:]
-            win[t, rest, CELLS:] = lo[SPAN:]
-
-    for t in range(5):
-        win[t, 6 * PACK:] = jnp.zeros((slots - 6 * PACK, 2 * CELLS), BF16)
-        gather(t, ax_keys, False)
-
     fix_keys = jnp.full((1, CELLS), -2.0, F32)
     for s in range(2):
         @pl.when(inside(ax, vt - steps[s]))
@@ -407,6 +371,42 @@
         keys = jnp.concatenate(keys, axis=1)
         for t in range(5):
             gather(t, keys, False)
+
+    for s in range(2):
+        for v in range(3):
+            @pl.when(inside(ax - steps[s], vt - (v - 1)))
+            def _():
+                axial(s, v, (ax - steps[s], vt - (v - 1))).wait_recv()
+    layer_keys = jnp.full((1, slots), -2.0, F32)
+    which = slot_row >> (SPAN.bit_length() - 1)
+    within = slot_row & (SPAN - 1)
+    for s in range(2):
+        for v in range(3):
+            w = s * 3 + v
+            base = (vt - (v - 1)) * total + (ax - steps[s]) * slots + (slots - SPAN if s == 0 else 0)
+            layer_keys = jnp.where(which == w, (within + base).astype(F32), layer_keys)
+    other_keys = jnp.full((1, CELLS), -2.0, F32)
+    for w in range(6):
+        row = ax_recv[w, 3 * PACK:3 * PACK + 1]
+        row = jnp.where(row > 0.0, row - 1.0, -2.0)
+        other_keys = jnp.where((lane1 >> 4) == w, row, other_keys)
+    ax_keys = jnp.concatenate([layer_keys[:, :6 * SPAN], other_keys], axis=1)
+
+    @pl.loop(0, 6)
+    def _(w):
+        tables = union_tables(*[ax_recv[w, r * PACK:(r + 1) * PACK] for r in range(3)])
+        layer = pl.ds(pl.multiple_of(w * SPAN, SPAN), SPAN)
+        rest = pl.ds(pl.multiple_of(6 * SPAN + w * MOVES, MOVES), MOVES)
+        for t in range(5):
+            hi, lo = halves(tables[t])
+            win[t, layer, :CELLS] = hi[:SPAN]
+            win[t, layer, CELLS:] = lo[:SPAN]
+            win[t, rest, :CELLS] = hi[SPAN:]
+            win[t, rest, CELLS:] = lo[SPAN:]
+
+    for t in range(5):
+        win[t, 6 * PACK:] = jnp.zeros((slots - 6 * PACK, 2 * CELLS), BF16)
+        gather(t, ax_keys, False)
 
     small = 32
 

time: 55.8 us -> 49.8 us (0.89)
  Pallas kernels: 48.4 us -> 42.5 us
    pallas_call x1, Pallas kernels: 48.4 us -> 42.5 us  [on_device(): pl.pallas_call(functools.partial(kernel, na, nv), out_shape=(jax.ShapeDty...]
where the time goes in v5:
time: 49.8 us; the launch traced here: 49.5 us
  Pallas kernels  42.5 us (85%)
  local copies, waits for them, and re-layouts  6.36 us (13%)
  between operations  0.66 us (1%)
    pallas_call x1, Pallas kernels, on_device(): pl.pallas_call(functools.partial(kernel, na, nv), out_shape=(jax.ShapeDty...  42.5 us
    unnamed x15, local copies, waits for them, and re-layouts  6.36 us

profile of v5, /device:TPU:1, one launch (start us, length us, event | category | flops | bytes accessed | tf_op | source)
XLA Modules:
  0.0 49.5 jit_solution(15910906107483422512)
XLA Ops:
  0.6 0.0 copy-start.3
  0.6 0.0 copy-start.4
  0.7 0.7 %copy.13 = s32[6,1,512]{2,0,1:T(8,128)S(1)} copy(s32[6,1,512]{2,1,0:T(1,128)} %param.11) | data formatting | bytes 24576
  1.4 0.0 copy-start.5
  1.4 0.0 copy-done.3
  1.4 0.0 copy-done.4
  1.4 0.6 %copy-done.5 = f32[4]{0:T(128)S(1)} copy-done((f32[4]{0:T(128)S(1)}, f32[4]{0:T(128)}, u32[]{:S(2)}) %copy-start.5) | copy-done | bytes 40
  2.0 0.0 copy-start
  2.0 1.2 %copy-done = f32[4,1,512,128]{3,2,1,0:T(8,128)S(1)} copy-done((f32[4,1,512,128]{3,2,1,0:T(8,128)S(1)}, f32[4,1,512,128]{3,2,1,0:T(8,128)}, u32[]{:S(2)}) %copy-start) | copy-done | bytes 1048600
  3.3 0.0 copy-start.1
  3.3 1.0 %copy-done.1 = f32[2,1,512,128]{3,2,1,0:T(8,128)S(1)} copy-done((f32[2,1,512,128]{3,2,1,0:T(8,128)S(1)}, f32[2,1,512,128]{3,2,1,0:T(8,128)}, u32[]{:S(2)}) %copy-start.1) | copy-done | bytes 524312
  4.3 0.0 copy-start.2
  4.3 0.9 %copy-done.2 = s32[1,512,128]{2,1,0:T(8,128)S(1)} copy-done((s32[1,512,128]{2,1,0:T(8,128)S(1)}, s32[1,512,128]{2,1,0:T(8,128)}, u32[]{:S(2)}) %copy-start.2) | copy-done | bytes 262168
  5.2 42.5 %shard_map.86 = (f32[2,512,128]{2,1,0:T(8,128)S(1)}, f32[4,512,128]{2,1,0:T(8,128)S(1)}) custom-call(f32[2,512,128]{2,1,0:T(8,128)S(1)} %bitcast.15, f32[4,512,128]{2,1,0:T(8,128)S(1)} %bitcast.12, s32[1,512]{1,0:T(1,128)S(1)} %copy-done.3, s32[1,512]{1,0:T(1,128)S(1)} %copy-done.4, s32[6,512]{1,0:T(8,128)S(1)} %bitcast.17, s32[512,128]{1,0:T(8,128)S(1)} %bitcast.16, ...), custom_call_target="tpu_custom_call" | custom-call | tf_op jit(solution)/shard_map/pallas_call | solution.py:470
  47.7 0.8 %copy.16 = f32[2,1,512,128]{3,2,1,0:T(8,128)} copy(f32[2,1,512,128]{3,2,1,0:T(8,128)S(1)} %bitcast.14) | data formatting | bytes 1048576
  48.5 1.0 %copy.17 = f32[4,1,512,128]{3,2,1,0:T(8,128)} copy(f32[4,1,512,128]{3,2,1,0:T(8,128)S(1)} %bitcast.13) | data formatting | bytes 2097152
Async XLA Ops:
  0.6 0.7 %copy-start.3 = (s32[1,512]{1,0:T(1,128)S(1)}, s32[1,512]{1,0:T(1,128)}, u32[]{:S(2)}) copy-start(s32[1,512]{1,0:T(1,128)} %home.1) | copy-start | bytes 6148
  0.6 0.7 %copy-start.4 = (s32[1,512]{1,0:T(1,128)S(1)}, s32[1,512]{1,0:T(1,128)}, u32[]{:S(2)}) copy-start(s32[1,512]{1,0:T(1,128)} %cnt.1) | copy-start | bytes 6148
  1.4 0.7 %copy-start.5 = (f32[4]{0:T(128)S(1)}, f32[4]{0:T(128)}, u32[]{:S(2)}) copy-start(f32[4]{0:T(128)} %rates.1) | copy-start | bytes 52
  2.0 1.2 %copy-start = (f32[4,1,512,128]{3,2,1,0:T(8,128)S(1)}, f32[4,1,512,128]{3,2,1,0:T(8,128)}, u32[]{:S(2)}) copy-start(f32[4,1,512,128]{3,2,1,0:T(8,128)} %param.8) | copy-start | bytes 3145732
  3.3 1.0 %copy-start.1 = (f32[2,1,512,128]{3,2,1,0:T(8,128)S(1)}, f32[2,1,512,128]{3,2,1,0:T(8,128)}, u32[]{:S(2)}) copy-start(f32[2,1,512,128]{3,2,1,0:T(8,128)} %param.7) | copy-start | bytes 1572868
  4.3 0.9 %copy-start.2 = (s32[1,512,128]{2,1,0:T(8,128)S(1)}, s32[1,512,128]{2,1,0:T(8,128)}, u32[]{:S(2)}) copy-start(s32[1,512,128]{2,1,0:T(8,128)} %param.12) | copy-start | bytes 786436
